TPU v7x, 128 devices: a whole 4x4x4 slice. The times are simulated.
128 devices in a mesh: row: 8 (over x, core), col: 16 (over y, z).
Axes of the slice: x: 4, y: 4, z: 4, core: 2. Of those that a mesh axis runs over, the one named last changes fastest.
Arguments:
- object_field: float32 [2, 4096, 8192], P(None, 'row', 'col'), may hold values from -5 to 5
- probe: float32 [2, 2, 256, 256], replicated, may hold values from -5 to 5
- amplitudes: float32 [1024, 256, 256], P(('row', 'col')), may hold values from 0 to 2.5
- positions: int32 [1024, 2], P(('row', 'col')), may hold values from 0 to 7936, as said below
- counts: int32 [128], P(('row', 'col')), may hold values from 1 to 8, as said below
Outputs:
- new_object: float32 [2, 4096, 8192], P(None, 'row', 'col')
- new_probe: float32 [2, 2, 256, 256], replicated
Inputs may be any that keep to these rules, and one draw needn't show every extreme that they name: `positions`: each slot's patch lies inside the object, and its top-left pixel lies in the tile of the device that holds the slot. `counts`: one device holds exactly 8 live slots in every draw; the others fewer.
All inputs are finite; a program needn't handle non-finite values.
Results may differ from a plain program's by a relative error of at most 0.0003.
Values sent between devices are 32-bit elements; how exact they have to be, the bound alone decides.
A program may use at most 256 MiB of HBM per device.

v0:
```python
import functools

import jax
import jax.numpy as jnp
import ml_dtypes
import numpy as np
from jax import lax
from jax.experimental import pallas as pl
from jax.experimental.pallas import tpu as pltpu
from jax.sharding import PartitionSpec as P

SIDE = 256
HALF = 128
MODES = 2
CHUNK = 32
VMEM_LIMIT = 56 * 1024 * 1024


def dft_tables():
    point = np.arange(HALF)[:, None]
    right, left = [], []
    for odd in (0, 1):
        angle = 2.0 * np.pi * ((point * (2 * np.arange(HALF)[None, :] + odd)) % SIDE) / SIDE
        cosine, sine = np.cos(angle) / 16.0, np.sin(angle) / 16.0
        table = np.block([[cosine, -sine], [sine, cosine]]).astype(np.float32)
        high = table.astype(ml_dtypes.bfloat16)
        low = (table - high.astype(np.float32)).astype(ml_dtypes.bfloat16)
        right += [np.concatenate([high, high, low], 0), np.concatenate([high.T, high.T, low.T], 0)]
        left += [np.concatenate([high.T, low.T, high.T], 1), np.concatenate([high, low, high], 1)]
    return np.stack(right), np.stack(left)


def split(value):
    high = value.astype(jnp.bfloat16)
    return high, (value - high.astype(jnp.float32)).astype(jnp.bfloat16)


def dot(left, right):
    return jnp.dot(left, right, preferred_element_type=jnp.float32)


def part(index):
    return pl.ds(index * HALF, HALF)


def pattern_kernel(
    span, order, corners, tile, right_upper, right_lower, lower_rim, corner_rim, probe, amplitude,
    right_table, left_table, grid, probe_sum,
    extended, sems, patch, rows_in, rows_out, columns_in, columns_out,
):
    copies = []
    for c in range(2):
        for j in range(6):
            if j < 4:
                pieces = ((tile, 0, 512), (lower_rim, 512, 256))
            else:
                pieces = ((right_upper, 0, 256), (right_lower, 256, 256), (corner_rim, 512, 256))
            for source, row, rows in pieces:
                copies.append((source.at[c, :, part(j % 4)], extended.at[c, j, pl.ds(row, rows)]))
    copies = [pltpu.make_async_copy(a, b, sems.at[k]) for k, (a, b) in enumerate(copies)]
    for copy in copies:
        copy.start()
    grid[...] = jnp.zeros_like(grid)
    probe_sum[...] = jnp.zeros_like(probe_sum)
    for copy in copies:
        copy.wait()

    lane = lax.broadcasted_iota(jnp.int32, (CHUNK, HALF), 1)

    def visit(step, carry):
        slot = order[step]
        top = corners[slot, 0]
        left = corners[slot, 1]
        first = left // HALF
        shift = lax.rem(left, HALF)
        back_shift = lax.rem(HALF - shift, HALF)

        def load(step, carry):
            r = pl.multiple_of(step * CHUNK, CHUNK)
            rows = pl.ds(r, CHUNK)
            pixels = []
            for c in range(2):
                tiles = [
                    pltpu.roll(extended[c, first + j, pl.ds(top + r, CHUNK), :], back_shift, 1) for j in range(3)
                ]
                pair = [jnp.where(lane < HALF - shift, tiles[j], tiles[j + 1]) for j in range(2)]
                for j in range(2):
                    patch[c, rows, part(j)] = pair[j]
                pixels.append(pair)
            for j in range(2):
                probe_sum[4, pl.ds(j * SIDE + r, CHUNK), :] += pixels[0][j] * pixels[0][j] + pixels[1][j] * pixels[1][j]
            for m in range(MODES):
                real, imag = [], []
                for j in range(2):
                    probe_real, probe_imag = probe[m, 0, rows, part(j)], probe[m, 1, rows, part(j)]
                    real.append(probe_real * pixels[0][j] - probe_imag * pixels[1][j])
                    imag.append(probe_real * pixels[1][j] + probe_imag * pixels[0][j])
                at = pl.ds(pl.multiple_of(m * SIDE + r, CHUNK), CHUNK)
                for k, (first_half, second_half) in enumerate((real, imag)):
                    for odd, value in enumerate((first_half + second_half, first_half - second_half)):
                        high, low = split(value)
                        rows_in[odd, at, part(k)] = high
                        rows_in[odd, at, part(2 + k)] = low
            return carry

        lax.fori_loop(0, SIDE // CHUNK, load, 0, unroll=True)

        def along_rows(inverse):
            for odd in range(2):
                cut = rows_in[odd]
                cut = jnp.concatenate([cut, cut[:, :SIDE]], axis=1)
                rows_out[odd] = dot(cut, right_table[2 * odd + inverse])

        def along_columns(inverse):
            for odd in range(2):
                high, low = columns_in[odd, 0], columns_in[odd, 1]
                cut = jnp.concatenate([high, high, low], axis=0)
                columns_out[odd] = dot(left_table[2 * odd + inverse], cut)

        along_rows(0)

        def turn(step, carry):
            r = pl.multiple_of(step * CHUNK, CHUNK)
            for m in range(MODES):
                for odd in range(2):
                    for k in range(2):
                        upper = rows_out[odd, pl.ds(m * SIDE + r, CHUNK), part(k)]
                        lower = rows_out[odd, pl.ds(m * SIDE + HALF + r, CHUNK), part(k)]
                        for q, value in enumerate((upper + lower, upper - lower)):
                            high, low = split(value)
                            columns_in[q, 0, pl.ds(k * HALF + r, CHUNK), part(2 * m + odd)] = high
                            columns_in[q, 1, pl.ds(k * HALF + r, CHUNK), part(2 * m + odd)] = low
            return carry

        lax.fori_loop(0, HALF // CHUNK, turn, 0, unroll=True)
        along_columns(0)

        def scale(step, carry):
            r = pl.multiple_of(step * CHUNK, CHUNK)
            for q in range(2):
                for odd in range(2):
                    values = [
                        [columns_out[q, pl.ds(k * HALF + r, CHUNK), part(2 * m + odd)] for k in range(2)]
                        for m in range(MODES)
                    ]
                    intensity = sum(v * v for pair in values for v in pair)
                    measured = amplitude[slot, pl.ds(q * HALF + r, CHUNK), part(odd)]
                    factor = measured * lax.rsqrt(jnp.maximum(intensity, 0.09)) - 1.0
                    for m in range(MODES):
                        for k in range(2):
                            high, low = split(values[m][k] * factor)
                            columns_in[q, 0, pl.ds(k * HALF + r, CHUNK), part(2 * m + odd)] = high
                            columns_in[q, 1, pl.ds(k * HALF + r, CHUNK), part(2 * m + odd)] = low
            return carry

        lax.fori_loop(0, HALF // CHUNK, scale, 0, unroll=True)
        along_columns(1)

        def turn_back(step, carry):
            r = pl.multiple_of(step * CHUNK, CHUNK)
            for m in range(MODES):
                for odd in range(2):
                    for k in range(2):
                        even_sum = columns_out[0, pl.ds(k * HALF + r, CHUNK), part(2 * m + odd)]
                        odd_sum = columns_out[1, pl.ds(k * HALF + r, CHUNK), part(2 * m + odd)]
                        for q, value in enumerate((even_sum + odd_sum, even_sum - odd_sum)):
                            high, low = split(value)
                            at = pl.ds(m * SIDE + q * HALF + r, CHUNK)
                            rows_in[odd, at, part(k)] = high
                            rows_in[odd, at, part(2 + k)] = low
            return carry

        lax.fori_loop(0, HALF // CHUNK, turn_back, 0, unroll=True)
        along_rows(1)

        def gather(step, carry):
            r = pl.multiple_of(step * CHUNK, CHUNK)
            rows = pl.ds(r, CHUNK)
            real_grad, imag_grad = [0.0, 0.0], [0.0, 0.0]
            for m in range(MODES):
                at = pl.ds(pl.multiple_of(m * SIDE + r, CHUNK), CHUNK)
                even = [rows_out[0, at, part(k)] for k in range(2)]
                odd = [rows_out[1, at, part(k)] for k in range(2)]
                for j in range(2):
                    real, imag = [e + o if j == 0 else e - o for e, o in zip(even, odd)]
                    patch_real, patch_imag = patch[0, rows, part(j)], patch[1, rows, part(j)]
                    probe_sum[2 * m, pl.ds(j * SIDE + r, CHUNK), :] += patch_real * real + patch_imag * imag
                    probe_sum[2 * m + 1, pl.ds(j * SIDE + r, CHUNK), :] += patch_real * imag - patch_imag * real
                    probe_real, probe_imag = probe[m, 0, rows, part(j)], probe[m, 1, rows, part(j)]
                    real_grad[j] += probe_real * real + probe_imag * imag
                    imag_grad[j] += probe_real * imag - probe_imag * real
            for c, pair in enumerate((real_grad, imag_grad)):
                here, there = [pltpu.roll(value, shift, 1) for value in pair]
                tiles = (
                    jnp.where(lane >= shift, here, 0.0),
                    jnp.where(lane >= shift, there, here),
                    jnp.where(lane >= shift, 0.0, there),
                )
                for j in range(3):
                    grid[c, first + j, pl.ds(top + r, CHUNK), :] += tiles[j]
            return carry

        lax.fori_loop(0, SIDE // CHUNK, gather, 0, unroll=True)
        return carry

    lax.fori_loop(span[0], span[1], visit, 0)


def patterns(span, order, corners, tile, right_upper, right_lower, lower_rim, corner_rim, probe, amplitude):
    right_table, left_table = dft_tables()
    smem, vmem, anywhere = [pl.BlockSpec(memory_space=s) for s in (pltpu.SMEM, pltpu.VMEM, pl.ANY)]
    return pl.pallas_call(
        pattern_kernel,
        out_shape=(
            jax.ShapeDtypeStruct((2, 6, 768, HALF), jnp.float32),
            jax.ShapeDtypeStruct((5, 2 * SIDE, HALF), jnp.float32),
        ),
        in_specs=[smem] * 3 + [anywhere] * 5 + [vmem] * 4,
        out_specs=(vmem, vmem),
        scratch_shapes=[
            pltpu.VMEM((2, 6, 768, HALF), jnp.float32),
            pltpu.SemaphoreType.DMA((28,)),
            pltpu.VMEM((2, SIDE, SIDE), jnp.float32),
            pltpu.VMEM((2, MODES * SIDE, 2 * SIDE), jnp.bfloat16),
            pltpu.VMEM((2, MODES * SIDE, SIDE), jnp.float32),
            pltpu.VMEM((2, 2, SIDE, MODES * SIDE), jnp.bfloat16),
            pltpu.VMEM((2, SIDE, MODES * SIDE), jnp.float32),
        ],
        compiler_params=pltpu.CompilerParams(vmem_limit_bytes=VMEM_LIMIT),
        cost_estimate=pl.CostEstimate(flops=5_000_000_000, bytes_accessed=20_000_000, transcendentals=0),
        name="patterns",
    )(span, order, corners, tile, right_upper, right_lower, lower_rim, corner_rim, probe, amplitude, right_table, left_table)


def prepare_kernel(corners, counts, probe, amplitude, parity, inverse_light, by_parity, canvas, power, columns):
    canvas[...] = jnp.zeros_like(canvas)
    power[...] = sum(probe[m, c] * probe[m, c] for m in range(MODES) for c in range(2))
    lane = lax.broadcasted_iota(jnp.int32, (CHUNK, HALF), 1)

    for source in range(4):

        def place(slot, carry):
            top = corners[source, slot, 0] + SIDE
            left = corners[source, slot, 1] + SIDE

            @pl.when((top > 0) & (left > 0))
            def _():
                first = left // HALF
                shift = lax.rem(left, HALF)
                for r in range(0, SIDE, CHUNK):
                    rows = pl.ds(r, CHUNK)
                    here, there = [pltpu.roll(power[rows, part(j)], shift, 1) for j in range(2)]
                    tiles = (
                        jnp.where(lane >= shift, here, 0.0),
                        jnp.where(lane >= shift, there, here),
                        jnp.where(lane >= shift, 0.0, there),
                    )
                    for j in range(3):
                        canvas[first + j, pl.ds(top + r, CHUNK), :] += tiles[j]

            return carry

        lax.fori_loop(0, counts[source], place, 0)

    for j in range(4):
        inverse_light[j] = 1.0 / (canvas[2 + j, pl.ds(SIDE, 512), :] + 1.0)

    def reorder(slot, carry):
        for j in range(2):
            columns[j] = amplitude[slot, :, part(j)]
        for q in range(2):
            value = jnp.concatenate([columns[j, pl.ds(q, HALF, stride=2), :] for j in range(2)], axis=1)
            pieces = []
            for _ in range(3):
                high = value.astype(jnp.bfloat16)
                pieces.append(high)
                value = value - high.astype(jnp.float32)
            by_parity[slot, part(q), :] = dot(jnp.concatenate(pieces, axis=1), parity[...])
        return carry

    lax.fori_loop(0, counts[0], reorder, 0)


def prepare(corners, counts, probe, amplitude):
    target = np.arange(SIDE)
    parity = (np.arange(SIDE)[:, None] == 2 * (target % HALF) + target // HALF).astype(ml_dtypes.bfloat16)
    smem, vmem = [pl.BlockSpec(memory_space=space) for space in (pltpu.SMEM, pltpu.VMEM)]
    return pl.pallas_call(
        prepare_kernel,
        out_shape=(
            jax.ShapeDtypeStruct((4, 512, HALF), jnp.float32),
            jax.ShapeDtypeStruct((8, SIDE, SIDE), jnp.float32),
        ),
        in_specs=[smem] * 2 + [vmem] * 3,
        out_specs=(vmem, vmem),
        scratch_shapes=[pltpu.VMEM((8, 1024, HALF), jnp.float32), pltpu.VMEM((SIDE, SIDE), jnp.float32), pltpu.VMEM((2, SIDE, HALF), jnp.float32)],
        compiler_params=pltpu.CompilerParams(vmem_limit_bytes=VMEM_LIMIT),
        cost_estimate=pl.CostEstimate(flops=2_000_000_000, bytes_accessed=8_000_000, transcendentals=0),
        name="prepare",
    )(corners, counts, probe, amplitude, np.concatenate([parity] * 3, 0))


def finish_kernel(
    grid, probe_sum, tile, inverse_light, probe, new_object, new_probe,
    own, own_half, inverse, old, corner_in, below_in, right_in, right_out, half_in, by_y, by_x, by_z, turned,
    local_sems, spill_send, spill_recv, half_send, half_recv, y_send, y_recv, x_send, x_recv, z_send, z_recv,
    x_back_send, x_back_recv, y_back_send, y_back_recv, last_send, last_recv,
):
    row, col = lax.axis_index("row"), lax.axis_index("col")
    x, core = row // 2, lax.rem(row, 2)
    y, z = col // 4, lax.rem(col, 4)
    sibling = (row + 1 - 2 * core, col)
    y_peers = {d: (row, lax.rem(y + d, 4) * 4 + z) for d in (1, 2, 3)}
    x_peers = {d: (lax.rem(x + d, 4) * 2 + core, col) for d in (1, 2, 3)}
    z_peers = {d: (row, y * 4 + lax.rem(z + d, 4)) for d in (1, 2, 3)}
    has_above, has_below = row > 0, row < 7
    has_left, has_right = col > 0, col < 15

    def remote(source, target, send, recv, device):
        return pltpu.make_async_remote_copy(
            src_ref=source, dst_ref=target, send_sem=send, recv_sem=recv, device_id=device,
            device_id_type=pl.DeviceIdType.MESH,
        )

    def signal(device):
        pl.semaphore_signal(barrier, inc=1, device_id=device, device_id_type=pl.DeviceIdType.MESH)

    half_at = core * 256
    loads = [
        pltpu.make_async_copy(probe_sum.at[:, pl.ds(pl.multiple_of(half_at, 256), 256)], own_half, local_sems.at[0]),
        pltpu.make_async_copy(grid.at[:, pl.ds(4, 2), pl.ds(0, 256)], right_out, local_sems.at[1]),
        pltpu.make_async_copy(grid.at[:, pl.ds(0, 4), pl.ds(0, 512)], own, local_sems.at[2]),
        pltpu.make_async_copy(inverse_light, inverse, local_sems.at[3]),
        pltpu.make_async_copy(tile, old, local_sems.at[4]),
    ]
    for load in loads:
        load.start()

    barrier = pltpu.get_barrier_semaphore()
    for device in [sibling, *y_peers.values(), *x_peers.values(), *z_peers.values()]:
        signal(device)
    steps = ((has_above, (row - 1, col)), (has_below, (row + 1, col)), (has_left, (row, col - 1)), (has_right, (row, col + 1)))
    for there, device in steps:
        pl.when(there)(functools.partial(signal, device))
    pl.semaphore_wait(barrier, 10 + sum(there.astype(jnp.int32) for there, _ in steps))

    below, right = (row + 1, col), (row, col + 1)
    corner = remote(
        grid.at[:, pl.ds(4, 2), pl.ds(512, 256)], corner_in, spill_send.at[0], spill_recv.at[0], below
    )
    right_lower = remote(
        grid.at[:, pl.ds(4, 2), pl.ds(256, 256)], right_in.at[:, :, pl.ds(256, 256)],
        spill_send.at[1], spill_recv.at[1], right,
    )
    lower = remote(grid.at[:, pl.ds(0, 4), pl.ds(512, 256)], below_in, spill_send.at[2], spill_recv.at[2], below)
    right_upper = remote(
        right_out, right_in.at[:, :, pl.ds(0, 256)], spill_send.at[3], spill_recv.at[3], right
    )

    def y_rows(d):
        return pl.ds(pl.multiple_of(lax.rem(y + d, 4) * 64, 64), 64)

    halves = {
        d: remote(
            probe_sum.at[:, pl.ds(pl.multiple_of((1 - core) * 256 + lax.rem(y + d, 4) * 64, 64), 64)],
            half_in.at[:, y_rows(d)], half_send.at[d], half_recv.at[d], sibling,
        )
        for d in range(4)
    }
    pl.when(has_below)(corner.start)
    for d in (2, 1, 3, 0):
        halves[d].start()
    pl.when(has_right)(right_lower.start)
    pl.when(has_below)(lower.start)

    loads[0].wait()
    outward = {
        d: remote(own_half.at[:, y_rows(d)], by_y.at[3 - d], y_send.at[d - 1], y_recv.at[3 - d], y_peers[d])
        for d in (1, 2, 3)
    }
    for d in (2, 1, 3, 0):
        halves[d].wait_recv()
        own_half[:, y_rows(d)] = own_half[:, y_rows(d)] + half_in[:, y_rows(d)]
        if d:
            outward[d].start()

    loads[1].wait()

    @pl.when(has_above)
    def _():
        corner.wait_recv()
        right_out[...] = right_out[...] + corner_in[...]

    pl.when(has_right)(right_upper.start)

    for d in (1, 2, 3):
        outward[d].wait_recv()
    mine = y_rows(0)
    own_half[:, mine] = own_half[:, mine] + (by_y[0] + by_y[1] + by_y[2])

    def x_rows(d, base):
        return pl.ds(pl.multiple_of(base + lax.rem(x + d, 4) * 16, 16), 16)

    crossing = {
        d: remote(own_half.at[:, x_rows(d, y * 64)], by_x.at[3 - d], x_send.at[d - 1], x_recv.at[3 - d], x_peers[d])
        for d in (1, 2, 3)
    }
    for d in (1, 2, 3):
        crossing[d].start()

    for load in loads[2:]:
        load.wait()

    def update(step, carry):
        rows = pl.ds(pl.multiple_of(step * CHUNK, CHUNK), CHUNK)
        for c in range(2):
            for j in range(4):
                new_object[c, rows, part(j)] = old[c, rows, part(j)] + own[c, j, rows] * inverse[j, rows]
        return carry

    lax.fori_loop(0, 512 // CHUNK, update, 0)

    for d in (1, 2, 3):
        crossing[d].wait_recv()
    by_z[z] = own_half[:, x_rows(0, y * 64)] + (by_x[0] + by_x[1] + by_x[2])
    along = {
        d: remote(by_z.at[z], by_z.at[z], z_send.at[d - 1], z_recv.at[3 - d], z_peers[d]) for d in (1, 2, 3)
    }
    for d in (1, 2, 3):
        along[d].start()
    for d in (1, 2, 3):
        along[d].wait_recv()
    total = (by_z[0] + by_z[1]) + (by_z[2] + by_z[3])
    light = total[4] + 1.0
    pixels = pl.ds(pl.multiple_of(y * 64 + x * 16, 16), 16)
    lanes = pl.ds(pl.multiple_of(core * HALF, HALF), HALF)
    home = x_rows(0, half_at + y * 64)
    for m in range(MODES):
        for c in range(2):
            turned[2 * m + c, home] = probe[m, c, pixels, lanes] + total[2 * m + c] / light

    back_x = {
        d: remote(turned.at[:, home], turned.at[:, home], x_back_send.at[d - 1], x_back_recv.at[3 - d], x_peers[d])
        for d in (1, 2, 3)
    }
    for d in (1, 2, 3):
        back_x[d].start()
    for d in (1, 2, 3):
        back_x[d].wait_recv()

    def quarter(d):
        return pl.ds(pl.multiple_of(half_at + lax.rem(y + d, 4) * 64, 64), 64)

    back_y = {
        d: remote(
            turned.at[:, quarter(0)], turned.at[:, quarter(0)], y_back_send.at[d - 1], y_back_recv.at[3 - d], y_peers[d]
        )
        for d in (1, 2, 3)
    }
    last = {
        d: remote(turned.at[:, quarter(d)], turned.at[:, quarter(d)], last_send.at[d], last_recv.at[d], sibling)
        for d in range(4)
    }
    for d in (1, 2, 3):
        back_y[d].start()
    last[0].start()
    for d in (1, 2, 3):
        back_y[4 - d].wait_recv()
        last[d].start()

    @pl.when(has_above)
    def _():
        lower.wait_recv()

        def add(step, carry):
            rows = pl.ds(pl.multiple_of(step * CHUNK, CHUNK), CHUNK)
            for c in range(2):
                for j in range(4):
                    new_object[c, rows, part(j)] += below_in[c, j, rows] * inverse[j, rows]
            return carry

        lax.fori_loop(0, SIDE // CHUNK, add, 0)

    @pl.when(has_left)
    def _():
        right_lower.wait_recv()
        right_upper.wait_recv()

        def add(step, carry):
            rows = pl.ds(pl.multiple_of(step * CHUNK, CHUNK), CHUNK)
            for c in range(2):
                for j in range(2):
                    new_object[c, rows, part(j)] += right_in[c, j, rows] * inverse[j, rows]
            return carry

        lax.fori_loop(0, 512 // CHUNK, add, 0)

    for d in range(4):
        last[d].wait_recv()
    for m in range(MODES):
        for c in range(2):
            for j in range(2):
                new_probe[m, c, :, part(j)] = turned[2 * m + c, pl.ds(j * SIDE, SIDE)]

    pl.when(has_below)(corner.wait_send)
    pl.when(has_below)(lower.wait_send)
    pl.when(has_right)(right_lower.wait_send)
    pl.when(has_right)(right_upper.wait_send)
    for copies in (halves, outward, crossing, along, back_x, back_y, last):
        for copy in copies.values():
            copy.wait_send()


def finish(grid, probe_sum, tile, inverse_light, probe):
    vmem, anywhere = [pl.BlockSpec(memory_space=space) for space in (pltpu.VMEM, pl.ANY)]
    f32 = functools.partial(pltpu.VMEM, dtype=jnp.float32)
    dma = pltpu.SemaphoreType.DMA
    return pl.pallas_call(
        finish_kernel,
        out_shape=(
            jax.ShapeDtypeStruct(tile.shape, jnp.float32),
            jax.ShapeDtypeStruct(probe.shape, jnp.float32),
        ),
        in_specs=[anywhere] * 4 + [vmem],
        out_specs=(vmem, vmem),
        scratch_shapes=[
            f32((2, 4, 512, HALF)),
            f32((5, 256, HALF)),
            f32((4, 512, HALF)),
            f32((2, 512, 512)),
            f32((2, 2, 256, HALF)),
            f32((2, 4, 256, HALF)),
            f32((2, 2, 512, HALF)),
            f32((2, 2, 256, HALF)),
            f32((5, 256, HALF)),
            f32((3, 5, 64, HALF)),
            f32((3, 5, 16, HALF)),
            f32((4, 5, 16, HALF)),
            f32((4, 512, HALF)),
            dma((5,)), dma((4,)), dma((4,)), dma((4,)), dma((4,)),
            *[dma((3,))] * 10,
            dma((4,)), dma((4,)),
        ],
        compiler_params=pltpu.CompilerParams(
            collective_id=0, has_side_effects=True, vmem_limit_bytes=VMEM_LIMIT
        ),
        name="finish",
    )(grid, probe_sum, tile, inverse_light, probe)


def shift_up(array, axis):
    count = lax.axis_size(axis)
    return lax.ppermute(array, axis, [(i, i - 1) for i in range(1, count)])


def shift_down(array, axis):
    count = lax.axis_size(axis)
    return lax.ppermute(array, axis, [(i, i + 1) for i in range(count - 1)])


def body(object_field, probe, amplitudes, positions, counts):
    tile_rows, tile_cols = object_field.shape[1:]
    right_upper = shift_up(object_field[:, :SIDE, :SIDE], "col")
    right_lower = shift_up(object_field[:, SIDE:, :SIDE], "col")
    lower_rim = shift_up(object_field[:, :SIDE, :], "row")
    corner_rim = shift_up(right_upper, "row")

    origin = jnp.stack([lax.axis_index("row") * tile_rows, lax.axis_index("col") * tile_cols])
    scans = jnp.concatenate([positions.reshape(-1), counts])
    scans = jnp.stack([scans, shift_down(scans, "col")])
    scans = jnp.concatenate([scans, shift_down(scans, "row")])
    corners = scans[:, :-1].reshape(4, -1, 2) - origin
    inverse_light, by_parity = prepare(corners, scans[:, -1], probe, amplitudes)

    span = jnp.stack([jnp.zeros((), jnp.int32), counts[0]])
    order = jnp.arange(positions.shape[0], dtype=jnp.int32)
    grid, probe_sum = patterns(
        span, order, corners[0], object_field, right_upper, right_lower, lower_rim, corner_rim, probe, by_parity
    )
    return finish(grid, probe_sum, object_field, inverse_light, probe)


def solution(mesh):
    in_specs = (
        P(None, "row", "col"),
        P(),
        P(("row", "col"), None, None),
        P(("row", "col"), None),
        P(("row", "col")),
    )
    out_specs = (P(None, "row", "col"), P())
    return jax.shard_map(body, mesh=mesh, in_specs=in_specs, out_specs=out_specs, check_vma=False)
```

profile of v0, /device:TPU:1, one launch (start us, length us, event | category | flops | bytes accessed | tf_op | source)
XLA Modules:
  0.0 133.5 jit_solution(8687056759514417155)
XLA Ops:
  0.6 0.0 copy-start
  1.4 0.8 copy.15
  2.2 0.1 reshape.11
  2.3 0.1 pad_add_fusion.3
  2.4 4.4 %collective-permute-start = (s32[17]{0:T(128)S(1)}, s32[17]{0:T(128)S(1)}, u32[]{:S(2)}, u32[]{:S(2)}) collective-permute-start(s32[17]{0:T(128)S(1)} %pad_add_fusion.3), channel_id=1, source_target_pairs={{0,1},{1,2},{2,3},{3,4},{4,5},{5,6},{6,7},{7,8},{8,9},{9,10},{10,1... | collective-permute-start | bytes 212 | tf_op jit(solution)/shard_map/ppermute | solution.py:558
  6.7 2.3 %fusion = (f32[2,256,256]{2,1,0:T(8,128)}, f32[2,256,256]{2,1,0:T(8,128)}) fusion(f32[2,512,512]{2,1,0:T(8,128)} %tile.3), kind=kLoop, calls=%fused_computation.8 | loop fusion | bytes 2097152 | tf_op jit(solution)/shard_map/slice | solution.py:564
  9.0 1.3 collective-permute-start.3
  10.3 1.3 collective-permute-start.2
  11.6 0.0 copy-done
  11.6 0.1 slice.22
  11.7 2.9 %collective-permute-start.4 = (f32[2,256,512]{2,1,0:T(8,128)S(1)}, f32[2,256,512]{2,1,0:T(8,128)S(1)}, u32[]{:S(2)}, u32[]{:S(2)}) collective-permute-start(f32[2,256,512]{2,1,0:T(8,128)S(1)} %slice.22), channel_id=1, source_target_pairs={{16,0},{32,16},{48,32},{64,48},{80,64},{96,80},{112,96},{17,1},{33... | collective-permute-start | bytes 3145736 | tf_op jit(solution)/shard_map/ppermute | solution.py:553
  14.6 0.1 fusion.1
  14.6 0.7 pad_add_fusion.2.span
  15.3 0.0 collective-permute-done
  15.3 3.0 %collective-permute-start.1 = (s32[2,17]{1,0:T(2,128)S(1)}, s32[2,17]{1,0:T(2,128)S(1)}, u32[]{:S(2)}, u32[]{:S(2)}) collective-permute-start(s32[2,17]{1,0:T(2,128)S(1)} %pad_add_fusion.1), channel_id=1, source_target_pairs={{0,16},{16,32},{32,48},{48,64},{64,80},{80,96},{96,112},{1,17},{17... | collective-permute-start | bytes 416 | tf_op jit(solution)/shard_map/ppermute | solution.py:558
  18.3 0.1 pad_add_fusion.4
  18.4 0.6 collective-permute-done.1
  19.0 0.1 copy.16
  19.1 0.1 copy.17
  19.3 16.1 %collective-permute-done.2.right_upper = f32[2,256,256]{2,1,0:T(8,128)} collective-permute-done((f32[2,256,256]{2,1,0:T(8,128)}, f32[2,256,256]{2,1,0:T(8,128)}, u32[]{:S(2)}, u32[]{:S(2)}) %collective-permute-start.2) | collective-permute-done | bytes 524320 | tf_op jit(solution)/shard_map/ppermute | solution.py:553
  35.3 3.5 %collective-permute-start.5 = (f32[2,256,256]{2,1,0:T(8,128)}, f32[2,256,256]{2,1,0:T(8,128)S(1)}, u32[]{:S(2)}, u32[]{:S(2)}) collective-permute-start(f32[2,256,256]{2,1,0:T(8,128)} %collective-permute-done.2.right_upper), channel_id=1, source_target_pairs={{16,0},{32,16},{48,32},{64,48},{80,64},{96,80},{112,96},{17,1},{33... | collective-permute-start | bytes 1572872 | tf_op jit(solution)/shard_map/ppermute | solution.py:553
  38.9 0.6 broadcast_subtract_fusion.corners
  39.5 0.7 slice_reduce_fusion.counts
  40.2 5.4 %prepare.1 = (f32[4,512,128]{2,1,0:T(8,128)}, f32[8,256,256]{2,1,0:T(8,128)}) custom-call(s32[4,8,2]{2,1,0:T(8,128)} %broadcast_subtract_fusion.corners, s32[4]{0:T(128)} %slice_reduce_fusion.counts, f32[2,2,256,256]{3,2,1,0:T(8,128)} %probe.5, f32[8,256,256]{2,1,0:T(8,128)} %amplitude.1, bf16[768,256]{1,0:T(8,128)(2,1)} %constant.19.clone.parity), custom_call_target="tpu_custom_call" | custom-call | flops 2000000000 | bytes 8000000 | tf_op jit(solution)/shard_map/prepare/pallas_call | solution.py:288
  45.6 1.3 slice_bitcast_fusion.corners
  46.8 0.0 collective-permute-done.3.right_lower
  46.8 0.2 collective-permute-done.5.corner_rim
  47.0 0.0 copy-start.3
  47.0 0.0 collective-permute-done.4.lower_rim
  47.0 0.0 copy-start.2
  47.0 0.6 iota.3.order
  47.7 0.1 copy-done.3
  47.8 0.4 copy-done.2
  48.2 14.3 %patterns.1 = (f32[2,6,768,128]{3,2,1,0:T(8,128)}, f32[5,512,128]{2,1,0:T(8,128)}) custom-call(s32[2]{0:T(128)} %pad_add_fusion.2.span, s32[8]{0:T(128)} %iota.3.order, s32[8,2]{1,0:T(8,128)} %slice_bitcast_fusion.corners, f32[2,512,512]{2,1,0:T(8,128)} %tile.3, f32[2,256,256]{2,1,0:T(8,128)} %collective-permute-done.2.right_upper, ...), custom_call_target="tpu_custom_call" | custom-call | flops 5000000000 | bytes 20000000 | tf_op jit(solution)/shard_map/patterns/pallas_call | solution.py:212
  62.5 66.8 %finish.1 = (f32[2,512,512]{2,1,0:T(8,128)}, f32[2,2,256,256]{3,2,1,0:T(8,128)}) custom-call(f32[2,6,768,128]{3,2,1,0:T(8,128)} %get-tuple-element.7.grid, f32[5,512,128]{2,1,0:T(8,128)} %get-tuple-element.8.probe_sum, f32[2,512,512]{2,1,0:T(8,128)} %tile.3, f32[4,512,128]{2,1,0:T(8,128)} %get-tuple-element.9.inverse_light, f32[2,2,256,256]{3,2,1,0:T(8,128)} %probe.5), custom_call_target="tpu_custom_call" | custom-call | tf_op jit(solution)/shard_map/finish/pallas_call | solution.py:518
  129.3 0.0 copy-start.1
  129.3 3.2 %copy.24 = f32[2,512,512]{2,1,0:T(8,128)} copy(f32[2,512,512]{2,1,0:T(8,128)} %get-tuple-element.14) | data formatting | bytes 4194304
  132.5 0.0 copy-done.1
  132.5 1.0 copy.25
  (2 shorter events, 0.0 us)
Async XLA Ops:
  0.6 11.0 %copy-start = (f32[2,512,512]{2,1,0:T(8,128)S(1)}, f32[2,512,512]{2,1,0:T(8,128)}, u32[]{:S(2)}) copy-start(f32[2,512,512]{2,1,0:T(8,128)} %tile.3) | copy-start | bytes 6291460
  2.4 12.9 %collective-permute-start = (s32[17]{0:T(128)S(1)}, s32[17]{0:T(128)S(1)}, u32[]{:S(2)}, u32[]{:S(2)}) collective-permute-start(s32[17]{0:T(128)S(1)} %pad_add_fusion.3), channel_id=1, source_target_pairs={{0,1},{1,2},{2,3},{3,4},{4,5},{5,6},{6,7},{7,8},{8,9},{9,10},{10,1... | collective-permute-start | bytes 212 | tf_op jit(solution)/shard_map/ppermute | solution.py:558
  9.0 37.8 %collective-permute-start.3 = (f32[2,256,256]{2,1,0:T(8,128)}, f32[2,256,256]{2,1,0:T(8,128)}, u32[]{:S(2)}, u32[]{:S(2)}) collective-permute-start(f32[2,256,256]{2,1,0:T(8,128)} %get-tuple-element.10), channel_id=1, source_target_pairs={{1,0},{2,1},{3,2},{4,3},{5,4},{6,5},{7,6},{8,7},{9,8},{10,9},{11,1... | collective-permute-start | bytes 1572872 | tf_op jit(solution)/shard_map/ppermute | solution.py:553
  10.3 25.0 %collective-permute-start.2 = (f32[2,256,256]{2,1,0:T(8,128)}, f32[2,256,256]{2,1,0:T(8,128)}, u32[]{:S(2)}, u32[]{:S(2)}) collective-permute-start(f32[2,256,256]{2,1,0:T(8,128)} %get-tuple-element.11), channel_id=1, source_target_pairs={{1,0},{2,1},{3,2},{4,3},{5,4},{6,5},{7,6},{8,7},{9,8},{10,9},{11,1... | collective-permute-start | bytes 1572872 | tf_op jit(solution)/shard_map/ppermute | solution.py:553
  11.7 35.4 %collective-permute-start.4 = (f32[2,256,512]{2,1,0:T(8,128)S(1)}, f32[2,256,512]{2,1,0:T(8,128)S(1)}, u32[]{:S(2)}, u32[]{:S(2)}) collective-permute-start(f32[2,256,512]{2,1,0:T(8,128)S(1)} %slice.22), channel_id=1, source_target_pairs={{16,0},{32,16},{48,32},{64,48},{80,64},{96,80},{112,96},{17,1},{33... | collective-permute-start | bytes 3145736 | tf_op jit(solution)/shard_map/ppermute | solution.py:553
  15.3 3.7 %collective-permute-start.1 = (s32[2,17]{1,0:T(2,128)S(1)}, s32[2,17]{1,0:T(2,128)S(1)}, u32[]{:S(2)}, u32[]{:S(2)}) collective-permute-start(s32[2,17]{1,0:T(2,128)S(1)} %pad_add_fusion.1), channel_id=1, source_target_pairs={{0,16},{16,32},{32,48},{48,64},{64,80},{80,96},{96,112},{1,17},{17... | collective-permute-start | bytes 416 | tf_op jit(solution)/shard_map/ppermute | solution.py:558
  35.3 11.7 %collective-permute-start.5 = (f32[2,256,256]{2,1,0:T(8,128)}, f32[2,256,256]{2,1,0:T(8,128)S(1)}, u32[]{:S(2)}, u32[]{:S(2)}) collective-permute-start(f32[2,256,256]{2,1,0:T(8,128)} %collective-permute-done.2.right_upper), channel_id=1, source_target_pairs={{16,0},{32,16},{48,32},{64,48},{80,64},{96,80},{112,96},{17,1},{33... | collective-permute-start | bytes 1572872 | tf_op jit(solution)/shard_map/ppermute | solution.py:553
  47.0 0.8 copy-start.3
  47.0 1.1 copy-start.2
  129.3 3.2 %copy-start.1 = (f32[2,2,256,256]{3,2,1,0:T(8,128)S(1)}, f32[2,2,256,256]{3,2,1,0:T(8,128)}, u32[]{:S(2)}) copy-start(f32[2,2,256,256]{3,2,1,0:T(8,128)} %get-tuple-element.15) | copy-start | bytes 3145732
where the time goes:
time: 134 us; the launch traced here: 133 us
  Pallas kernels  86.5 us (65%)
  waiting for transfers between devices  16.9 us (13%)
  starting transfers between devices  16.4 us (12%)
  local copies, waits for them, and re-layouts  10.7 us (8%)
  between operations  1.54 us (1%)
  other arithmetic  1.51 us (1%)
    pallas_call x1, Pallas kernels, finish(): pl.pallas_call(finish_kernel, out_shape=(jax.ShapeDtypeStruct(tile.shape,...  66.8 us
    ppermute x4, waiting for transfers between devices, shift_up(): return lax.ppermute(array, axis, [(i, i - 1) for i in range(1, count)])  16.2 us
    pallas_call x1, Pallas kernels, patterns(): pl.pallas_call(pattern_kernel, out_shape=(jax.ShapeDtypeStruct((2, 6, 768...  14.3 us
    ppermute x4, starting transfers between devices, shift_up(): return lax.ppermute(array, axis, [(i, i - 1) for i in range(1, count)])  8.98 us
    ppermute x2, starting transfers between devices, shift_down(): return lax.ppermute(array, axis, [(i, i + 1) for i in range(count - 1)])  7.38 us
    pallas_call x1, Pallas kernels, prepare(): pl.pallas_call(prepare_kernel, out_shape=(jax.ShapeDtypeStruct((4, 512, H...  5.4 us
    unnamed x11, local copies, waits for them, and re-layouts  5.4 us
  transfers between devices with their start and end apart: 6, of which 3 were waited for; matrix products, arithmetic and copies ran while one was open for 4% of the time, Pallas kernels for 4%

commit v1 on v0

v1 whole, which is shorter than its diff:
```python
import functools

import jax
import jax.numpy as jnp
import ml_dtypes
import numpy as np
from jax import lax
from jax.experimental import pallas as pl
from jax.experimental.pallas import tpu as pltpu
from jax.sharding import PartitionSpec as P

SIDE = 256
HALF = 128
MODES = 2
CHUNK = 32
VMEM_LIMIT = 56 * 1024 * 1024


def dft_tables():
    point = np.arange(HALF)[:, None]
    tables = []
    for odd in (0, 1):
        angle = 2.0 * np.pi * ((point * (2 * np.arange(HALF)[None, :] + odd)) % SIDE) / SIDE
        cosine, sine = np.cos(angle) / 16.0, np.sin(angle) / 16.0
        table = np.block([[cosine, -sine], [sine, cosine]]).astype(np.float32)
        tables += [table, table.T]
    return np.stack(tables)


def split(value):
    high = value.astype(jnp.bfloat16)
    return high, (value - high.astype(jnp.float32)).astype(jnp.bfloat16)


def dot(left, right):
    return jnp.dot(left, right, preferred_element_type=jnp.float32)


def part(index):
    return pl.ds(index * HALF, HALF)


def pattern_kernel(
    positions, counts, tile, right_rim, lower_rim, probe_in, amplitude_in, tables_in, grid, probe_sum,
    extended, probe, amplitude, tables, right_table, left_table, sems,
    patch, rows_in, rows_out, columns_in, columns_out,
):
    copies = [(tile.at[c, :, part(j)], extended.at[c, j, pl.ds(0, 512)]) for c in range(2) for j in range(4)]
    copies.append((right_rim, extended.at[:, pl.ds(4, 2)]))
    copies.append((lower_rim, extended.at[:, pl.ds(0, 4), pl.ds(512, 256)]))
    copies += [(tables_in, tables), (probe_in, probe), (amplitude_in, amplitude)]
    copies = [pltpu.make_async_copy(a, b, sems.at[k]) for k, (a, b) in enumerate(copies)]
    for copy in copies[-3:] + copies[:-3]:
        copy.start()
    grid[...] = jnp.zeros_like(grid)
    probe_sum[...] = jnp.zeros_like(probe_sum)
    copies[-3].wait()
    for k in range(4):
        high, low = split(tables[k])
        for piece, value in enumerate((high, high, low)):
            right_table[k, pl.ds(piece * SIDE, SIDE)] = value
        for piece, value in enumerate((high, low, high)):
            left_table[k ^ 1, :, pl.ds(piece * SIDE, SIDE)] = value
    for copy in copies[:-3] + copies[-2:]:
        copy.wait()

    lane = lax.broadcasted_iota(jnp.int32, (CHUNK, HALF), 1)

    row_start, col_start = lax.axis_index("row") * 512, lax.axis_index("col") * 512

    def phases(slot, live, patch, rows_in, rows_out, columns_in, columns_out):
        top = positions[slot, 0] - row_start
        left = positions[slot, 1] - col_start
        first = left // HALF
        shift = lax.rem(left, HALF)
        back_shift = lax.rem(HALF - shift, HALF)

        def load(step, carry):
            r = pl.multiple_of(step * CHUNK, CHUNK)
            rows = pl.ds(r, CHUNK)
            pixels = []
            for c in range(2):
                tiles = [
                    pltpu.roll(extended[c, first + j, pl.ds(top + r, CHUNK), :], back_shift, 1) for j in range(3)
                ]
                pair = [jnp.where(lane < HALF - shift, tiles[j], tiles[j + 1]) for j in range(2)]
                for j in range(2):
                    patch[c, rows, part(j)] = pair[j]
                pixels.append(pair)
            for j in range(2):
                probe_sum[4, pl.ds(j * SIDE + r, CHUNK), :] += live * (pixels[0][j] * pixels[0][j] + pixels[1][j] * pixels[1][j])
            for m in range(MODES):
                real, imag = [], []
                for j in range(2):
                    probe_real, probe_imag = probe[m, 0, rows, part(j)], probe[m, 1, rows, part(j)]
                    real.append(probe_real * pixels[0][j] - probe_imag * pixels[1][j])
                    imag.append(probe_real * pixels[1][j] + probe_imag * pixels[0][j])
                at = pl.ds(pl.multiple_of(m * SIDE + r, CHUNK), CHUNK)
                for k, (first_half, second_half) in enumerate((real, imag)):
                    for odd, value in enumerate((first_half + second_half, first_half - second_half)):
                        high, low = split(value)
                        rows_in[odd, at, part(k)] = high
                        rows_in[odd, at, part(2 + k)] = low
            return carry

        lax.fori_loop(0, SIDE // CHUNK, load, 0, unroll=True)
        yield

        def along_rows(inverse):
            for odd in range(2):
                cut = rows_in[odd]
                cut = jnp.concatenate([cut, cut[:, :SIDE]], axis=1)
                rows_out[odd] = dot(cut, right_table[2 * odd + inverse])

        def along_columns(inverse):
            for odd in range(2):
                high, low = columns_in[odd, 0], columns_in[odd, 1]
                cut = jnp.concatenate([high, high, low], axis=0)
                columns_out[odd] = dot(left_table[2 * odd + inverse], cut)

        along_rows(0)
        yield

        def turn(step, carry):
            r = pl.multiple_of(step * CHUNK, CHUNK)
            for m in range(MODES):
                for odd in range(2):
                    for k in range(2):
                        upper = rows_out[odd, pl.ds(m * SIDE + r, CHUNK), part(k)]
                        lower = rows_out[odd, pl.ds(m * SIDE + HALF + r, CHUNK), part(k)]
                        for q, value in enumerate((upper + lower, upper - lower)):
                            high, low = split(value)
                            columns_in[q, 0, pl.ds(k * HALF + r, CHUNK), part(2 * m + odd)] = high
                            columns_in[q, 1, pl.ds(k * HALF + r, CHUNK), part(2 * m + odd)] = low
            return carry

        lax.fori_loop(0, HALF // CHUNK, turn, 0, unroll=True)
        yield
        along_columns(0)
        yield

        def scale(step, carry):
            r = pl.multiple_of(step * CHUNK, CHUNK)
            for q in range(2):
                for odd in range(2):
                    values = [
                        [columns_out[q, pl.ds(k * HALF + r, CHUNK), part(2 * m + odd)] for k in range(2)]
                        for m in range(MODES)
                    ]
                    intensity = sum(v * v for pair in values for v in pair)
                    measured = amplitude[slot, pl.ds(q * HALF + r, CHUNK), part(odd)]
                    factor = live * (measured * lax.rsqrt(jnp.maximum(intensity, 0.09)) - 1.0)
                    for m in range(MODES):
                        for k in range(2):
                            high, low = split(values[m][k] * factor)
                            columns_in[q, 0, pl.ds(k * HALF + r, CHUNK), part(2 * m + odd)] = high
                            columns_in[q, 1, pl.ds(k * HALF + r, CHUNK), part(2 * m + odd)] = low
            return carry

        lax.fori_loop(0, HALF // CHUNK, scale, 0, unroll=True)
        yield
        along_columns(1)
        yield

        def turn_back(step, carry):
            r = pl.multiple_of(step * CHUNK, CHUNK)
            for m in range(MODES):
                for odd in range(2):
                    for k in range(2):
                        even_sum = columns_out[0, pl.ds(k * HALF + r, CHUNK), part(2 * m + odd)]
                        odd_sum = columns_out[1, pl.ds(k * HALF + r, CHUNK), part(2 * m + odd)]
                        for q, value in enumerate((even_sum + odd_sum, even_sum - odd_sum)):
                            high, low = split(value)
                            at = pl.ds(m * SIDE + q * HALF + r, CHUNK)
                            rows_in[odd, at, part(k)] = high
                            rows_in[odd, at, part(2 + k)] = low
            return carry

        lax.fori_loop(0, HALF // CHUNK, turn_back, 0, unroll=True)
        yield
        along_rows(1)
        yield

        def gather(step, carry):
            r = pl.multiple_of(step * CHUNK, CHUNK)
            rows = pl.ds(r, CHUNK)
            real_grad, imag_grad = [0.0, 0.0], [0.0, 0.0]
            for m in range(MODES):
                at = pl.ds(pl.multiple_of(m * SIDE + r, CHUNK), CHUNK)
                even = [rows_out[0, at, part(k)] for k in range(2)]
                odd = [rows_out[1, at, part(k)] for k in range(2)]
                for j in range(2):
                    real, imag = [e + o if j == 0 else e - o for e, o in zip(even, odd)]
                    patch_real, patch_imag = patch[0, rows, part(j)], patch[1, rows, part(j)]
                    probe_sum[2 * m, pl.ds(j * SIDE + r, CHUNK), :] += patch_real * real + patch_imag * imag
                    probe_sum[2 * m + 1, pl.ds(j * SIDE + r, CHUNK), :] += patch_real * imag - patch_imag * real
                    probe_real, probe_imag = probe[m, 0, rows, part(j)], probe[m, 1, rows, part(j)]
                    real_grad[j] += probe_real * real + probe_imag * imag
                    imag_grad[j] += probe_real * imag - probe_imag * real
            for c, pair in enumerate((real_grad, imag_grad)):
                here, there = [pltpu.roll(value, shift, 1) for value in pair]
                tiles = (
                    jnp.where(lane >= shift, here, 0.0),
                    jnp.where(lane >= shift, there, here),
                    jnp.where(lane >= shift, 0.0, there),
                )
                for j in range(3):
                    grid[c, first + j, pl.ds(top + r, CHUNK), :] += tiles[j]
            return carry

        lax.fori_loop(0, SIDE // CHUNK, gather, 0, unroll=True)
        yield

    def visit(step, carry):
        pair = []
        for k in range(2):
            live = jnp.where(2 * step + k < counts[0], 1.0, 0.0)
            pair.append(phases(2 * step + k, live, *(buffer.at[k] for buffer in (patch, rows_in, rows_out, columns_in, columns_out))))
        next(pair[0])
        for _ in pair[0]:
            next(pair[1])
        for _ in pair[1]:
            pass
        return carry

    lax.fori_loop(0, (counts[0] + 1) // 2, visit, 0)


def patterns(positions, counts, tile, right_rim, lower_rim, probe, amplitude):
    tables = dft_tables()
    smem, vmem, anywhere = [pl.BlockSpec(memory_space=s) for s in (pltpu.SMEM, pltpu.VMEM, pl.ANY)]
    f32 = functools.partial(pltpu.VMEM, dtype=jnp.float32)
    bf16 = functools.partial(pltpu.VMEM, dtype=jnp.bfloat16)
    return pl.pallas_call(
        pattern_kernel,
        out_shape=(
            jax.ShapeDtypeStruct((2, 6, 768, HALF), jnp.float32),
            jax.ShapeDtypeStruct((5, 2 * SIDE, HALF), jnp.float32),
        ),
        in_specs=[smem] * 2 + [anywhere] * 6,
        out_specs=(vmem, vmem),
        scratch_shapes=[
            f32((2, 6, 768, HALF)),
            f32(probe.shape),
            f32(amplitude.shape),
            f32(tables.shape),
            bf16((4, 3 * SIDE, SIDE)),
            bf16((4, SIDE, 3 * SIDE)),
            pltpu.SemaphoreType.DMA((13,)),
            f32((2, 2, SIDE, SIDE)),
            bf16((2, 2, MODES * SIDE, 2 * SIDE)),
            f32((2, 2, MODES * SIDE, SIDE)),
            bf16((2, 2, 2, SIDE, MODES * SIDE)),
            f32((2, 2, SIDE, MODES * SIDE)),
        ],
        compiler_params=pltpu.CompilerParams(vmem_limit_bytes=VMEM_LIMIT),
        cost_estimate=pl.CostEstimate(flops=5_000_000_000, bytes_accessed=20_000_000, transcendentals=0),
        name="patterns",
    )(positions, counts, tile, right_rim, lower_rim, probe, amplitude, tables)


MESH_ID = pl.DeviceIdType.MESH


def remote(source, target, send, recv, device):
    return pltpu.make_async_remote_copy(
        src_ref=source, dst_ref=target, send_sem=send, recv_sem=recv, device_id=device, device_id_type=MESH_ID
    )


def rims_kernel(
    positions, counts, tile, probe, amplitude, right_rim, lower_rim, inverse_light, by_parity,
    parity, canvas, light, measured, reordered, columns, scan_in, scan, local_sems,
    upper_send, upper_recv, under_send, under_recv, lower_send, lower_recv, corner_send, corner_recv,
    scan_send, scan_recv,
):
    row, col = lax.axis_index("row"), lax.axis_index("col")
    has_above, has_below = row > 0, row < 7
    has_left, has_right = col > 0, col < 15
    above, below, left, right = (row - 1, col), (row + 1, col), (row, col - 1), (row, col + 1)
    partners = (
        (has_above, above), (has_below, below), (has_left, left), (has_right, right),
        (has_above & has_left, (row - 1, col - 1)), (has_below & has_right, (row + 1, col + 1)),
    )
    barrier = pltpu.get_barrier_semaphore()
    for there, device in partners:

        @pl.when(there)
        def _():
            pl.semaphore_signal(barrier, inc=1, device_id=device, device_id_type=MESH_ID)

    load = pltpu.make_async_copy(amplitude, measured, local_sems.at[1])
    load.start()
    slot_of = lax.broadcasted_iota(jnp.int32, (8, HALF), 0)
    field = lax.broadcasted_iota(jnp.int32, (8, HALF), 1)
    own_scan = jnp.where(slot_of < counts[0], 1, 0)
    for slot in range(8):
        for k in range(2):
            own_scan = jnp.where((slot_of == slot) & (field == k), positions[slot, k], own_scan)
    scan_in[0] = own_scan
    pl.semaphore_wait(barrier, sum(there.astype(jnp.int32) for there, _ in partners))

    pieces = [(c, j) for c in range(2) for j in range(2)]
    upper = [
        remote(
            tile.at[c, pl.ds(0, 256), part(j)], right_rim.at[c, j, pl.ds(0, 256)], upper_send.at[k], upper_recv.at[k], left
        )
        for k, (c, j) in enumerate(pieces)
    ]
    under = [
        remote(
            tile.at[c, pl.ds(256, 256), part(j)], right_rim.at[c, j, pl.ds(256, 256)],
            under_send.at[k], under_recv.at[k], left,
        )
        for k, (c, j) in enumerate(pieces)
    ]
    lower = [
        remote(
            tile.at[c, pl.ds(0, 256), part(j)], lower_rim.at[c, j],
            lower_send.at[4 * c + j], lower_recv.at[4 * c + j], above,
        )
        for c in range(2) for j in range(4)
    ]
    corner = remote(
        right_rim.at[:, :, pl.ds(0, 256)], right_rim.at[:, :, pl.ds(512, 256)],
        corner_send.at[0], corner_recv.at[0], above,
    )
    sources = (
        (has_right, right, has_left),
        (has_below, below, has_above),
        (has_below & has_right, (row + 1, col + 1), has_above & has_left),
    )
    passed = [
        remote(scan_in.at[0], scan_in.at[1 + k], scan_send.at[k], scan_recv.at[k], device)
        for k, (_, device, _) in enumerate(sources)
    ]

    @pl.when(has_left)
    def _():
        for copy in upper:
            copy.start()

    for copy, (there, _, arrives) in zip(passed, sources):
        pl.when(there)(copy.start)

    @pl.when(has_above)
    def _():
        for copy in lower:
            copy.start()

    @pl.when(has_left)
    def _():
        for copy in under:
            copy.start()

    line = lax.broadcasted_iota(jnp.int32, (3 * SIDE, SIDE), 0) % SIDE
    target = lax.broadcasted_iota(jnp.int32, (3 * SIDE, SIDE), 1)
    parity[...] = jnp.where(line == 2 * (target % HALF) + target // HALF, 1.0, 0.0).astype(jnp.bfloat16)
    load.wait()

    def reorder(slot, carry):
        for j in range(2):
            columns[j] = measured[slot, :, part(j)]
        for q in range(2):
            value = jnp.concatenate([columns[j, pl.ds(q, HALF, stride=2), :] for j in range(2)], axis=1)
            cut = []
            for _ in range(3):
                high = value.astype(jnp.bfloat16)
                cut.append(high)
                value = value - high.astype(jnp.float32)
            reordered[slot, part(q), :] = dot(jnp.concatenate(cut, axis=1), parity[...])
        return carry

    lax.fori_loop(0, 8, reorder, 0)
    stores = [pltpu.make_async_copy(reordered, by_parity, local_sems.at[1])]
    stores[0].start()

    canvas[...] = jnp.zeros_like(canvas)
    for j in range(2):
        canvas[4 + j, pl.ds(512, SIDE), :] = sum(probe[m, c, :, part(j)] * probe[m, c, :, part(j)] for m in range(MODES) for c in range(2))
    light[...] = jnp.zeros_like(light)
    for copy, (there, _, arrives), k in zip(passed, sources, range(1, 4)):
        pl.when(arrives)(copy.wait_recv)

        @pl.when(jnp.logical_not(arrives))
        def _():
            scan_in[k] = jnp.zeros_like(scan_in[k])

    to_scalars = pltpu.make_async_copy(scan_in, scan, local_sems.at[2])
    to_scalars.start()
    to_scalars.wait()
    lane = lax.broadcasted_iota(jnp.int32, (CHUNK, HALF), 1)

    def shine(source, height, width, slot, carry):
        top = scan[source, slot, 0] - row * 512
        start = 512 - (scan[source, slot, 1] - col * 512)
        live = scan[source, slot, 2] > 0
        top = jnp.where(live, 512 - top, 1024)
        start = jnp.where(live, start, 0)
        first = start // HALF
        shift = lax.rem(start, HALF)
        back_shift = lax.rem(HALF - shift, HALF)

        def rows_of(step, carry):
            r = pl.multiple_of(step * CHUNK, CHUNK)
            tiles = [pltpu.roll(canvas[first + j, pl.ds(top + r, CHUNK), :], back_shift, 1) for j in range(width + 1)]
            for j in range(width):
                light[j, pl.ds(r, CHUNK), :] += jnp.where(lane < HALF - shift, tiles[j], tiles[j + 1])
            return carry

        lax.fori_loop(0, height // CHUNK, rows_of, 0, unroll=4)
        return carry

    lax.fori_loop(0, 8, functools.partial(shine, 0, 512, 4), 0)

    @pl.when(has_right)
    def _():
        for copy in upper:
            copy.wait_recv()

    pl.when(has_right & has_above)(corner.start)

    lax.fori_loop(0, 8, functools.partial(shine, 1, 512, 2), 0)
    lax.fori_loop(0, 8, functools.partial(shine, 2, 256, 4), 0)
    lax.fori_loop(0, 8, functools.partial(shine, 3, 256, 2), 0)
    light[...] = 1.0 / (light[...] + 1.0)
    stores.append(pltpu.make_async_copy(light, inverse_light, local_sems.at[3]))
    stores[1].start()

    @pl.when(has_below)
    def _():
        for copy in lower:
            copy.wait_recv()

    @pl.when(has_right)
    def _():
        for copy in under:
            copy.wait_recv()

    pl.when(has_right & has_below)(corner.wait_recv)

    for store in stores:
        store.wait()
    for copy, (there, _, _) in zip(passed, sources):
        pl.when(there)(copy.wait_send)

    @pl.when(has_left)
    def _():
        for copy in upper + under:
            copy.wait_send()

    @pl.when(has_above)
    def _():
        for copy in lower:
            copy.wait_send()

    pl.when(has_right & has_above)(corner.wait_send)


def rims(positions, counts, tile, probe, amplitude):
    smem, vmem, anywhere = [pl.BlockSpec(memory_space=space) for space in (pltpu.SMEM, pltpu.VMEM, pl.ANY)]
    f32 = functools.partial(pltpu.VMEM, dtype=jnp.float32)
    dma = pltpu.SemaphoreType.DMA
    return pl.pallas_call(
        rims_kernel,
        out_shape=(
            jax.ShapeDtypeStruct((2, 2, 768, HALF), jnp.float32),
            jax.ShapeDtypeStruct((2, 4, 256, HALF), jnp.float32),
            jax.ShapeDtypeStruct((4, 512, HALF), jnp.float32),
            jax.ShapeDtypeStruct(amplitude.shape, jnp.float32),
        ),
        in_specs=[smem, smem, anywhere, vmem, anywhere],
        out_specs=(anywhere,) * 4,
        scratch_shapes=[
            pltpu.VMEM((3 * SIDE, SIDE), jnp.bfloat16),
            f32((13, 1536, HALF)),
            f32((4, 512, HALF)),
            f32(amplitude.shape),
            f32(amplitude.shape),
            f32((2, SIDE, HALF)),
            pltpu.VMEM((4, 8, HALF), jnp.int32),
            pltpu.SMEM((4, 8, HALF), jnp.int32),
            dma((4,)),
            dma((4,)), dma((4,)), dma((4,)), dma((4,)), dma((8,)), dma((8,)), dma((1,)), dma((1,)), dma((3,)), dma((3,)),
        ],
        compiler_params=pltpu.CompilerParams(
            collective_id=1, has_side_effects=True, vmem_limit_bytes=VMEM_LIMIT
        ),
        name="rims",
    )(positions, counts, tile, probe, amplitude)


def finish_kernel(
    grid, probe_sum, tile, inverse_light, probe, new_object, turned,
    own, own_half, inverse, old, corner_in, below_in, right_in, right_out, half_in, by_y, by_xz,
    local_sems, spill_send, spill_recv, half_send, half_recv, y_send, y_recv, xz_send, xz_recv,
    xz_back_send, xz_back_recv, y_back_send, y_back_recv, last_send, last_recv,
):
    row, col = lax.axis_index("row"), lax.axis_index("col")
    x, core = row // 2, lax.rem(row, 2)
    y, z = col // 4, lax.rem(col, 4)
    sibling = (row + 1 - 2 * core, col)
    y_peers = {d: (row, lax.rem(y + d, 4) * 4 + z) for d in (1, 2, 3)}
    xz_peers = {4 * dx + dz: (lax.rem(x + dx, 4) * 2 + core, y * 4 + lax.rem(z + dz, 4)) for dx in range(4) for dz in range(4)}
    del xz_peers[0]
    twin = x + 1 - 2 * lax.rem(x, 2)
    set_peers = {
        4 * flip + dz: ((twin if flip else x) * 2 + core, y * 4 + lax.rem(z + dz, 4)) for flip in range(2) for dz in range(4)
    }
    del set_peers[0]
    has_above, has_below = row > 0, row < 7
    has_left, has_right = col > 0, col < 15

    def signal(device):
        pl.semaphore_signal(barrier, inc=1, device_id=device, device_id_type=pl.DeviceIdType.MESH)

    half_at = core * 256
    loads = [
        pltpu.make_async_copy(probe_sum.at[:, pl.ds(pl.multiple_of(half_at, 256), 256)], own_half, local_sems.at[0]),
        pltpu.make_async_copy(grid.at[:, pl.ds(4, 2), pl.ds(0, 256)], right_out, local_sems.at[1]),
        pltpu.make_async_copy(grid.at[:, pl.ds(0, 4), pl.ds(0, 512)], own, local_sems.at[2]),
        pltpu.make_async_copy(inverse_light, inverse, local_sems.at[3]),
        pltpu.make_async_copy(tile, old, local_sems.at[4]),
    ]
    for load in loads:
        load.start()

    barrier = pltpu.get_barrier_semaphore()
    for device in [sibling, *y_peers.values(), *xz_peers.values()]:
        signal(device)
    steps = ((has_above, (row - 1, col)), (has_below, (row + 1, col)), (has_left, (row, col - 1)), (has_right, (row, col + 1)))
    for there, device in steps:
        pl.when(there)(functools.partial(signal, device))
    pl.semaphore_wait(barrier, 19 + sum(there.astype(jnp.int32) for there, _ in steps))

    below, right = (row + 1, col), (row, col + 1)
    corner = remote(
        grid.at[:, pl.ds(4, 2), pl.ds(512, 256)], corner_in, spill_send.at[0], spill_recv.at[0], below
    )
    right_lower = remote(
        grid.at[:, pl.ds(4, 2), pl.ds(256, 256)], right_in.at[:, :, pl.ds(256, 256)],
        spill_send.at[1], spill_recv.at[1], right,
    )
    lower = remote(grid.at[:, pl.ds(0, 4), pl.ds(512, 256)], below_in, spill_send.at[2], spill_recv.at[2], below)
    right_upper = remote(
        right_out, right_in.at[:, :, pl.ds(0, 256)], spill_send.at[3], spill_recv.at[3], right
    )

    def y_rows(d):
        return pl.ds(pl.multiple_of(lax.rem(y + d, 4) * 64, 64), 64)

    halves = {
        d: remote(
            probe_sum.at[:, pl.ds(pl.multiple_of((1 - core) * 256 + lax.rem(y + d, 4) * 64, 64), 64)],
            half_in.at[:, y_rows(d)], half_send.at[d], half_recv.at[d], sibling,
        )
        for d in range(4)
    }
    pl.when(has_below)(corner.start)
    for d in (2, 1, 3, 0):
        halves[d].start()
    pl.when(has_right)(right_lower.start)

    loads[0].wait()
    outward = {
        d: remote(own_half.at[:, y_rows(d)], by_y.at[3 - d], y_send.at[d - 1], y_recv.at[3 - d], y_peers[d])
        for d in (1, 2, 3)
    }
    for d in (2, 1, 3, 0):
        halves[d].wait_recv()
        own_half[:, y_rows(d)] = own_half[:, y_rows(d)] + half_in[:, y_rows(d)]
        if d:
            outward[d].start()

    loads[1].wait()

    @pl.when(has_above)
    def _():
        corner.wait_recv()
        right_out[...] = right_out[...] + corner_in[...]

    pl.when(has_right)(right_upper.start)
    pl.when(has_below)(lower.start)

    for d in (1, 2, 3):
        outward[d].wait_recv()
    mine = y_rows(0)
    own_half[:, mine] = own_half[:, mine] + (by_y[0] + by_y[1] + by_y[2])

    def eighth(index, base):
        return pl.ds(pl.multiple_of(base + index * 8, 8), 8)

    me, group = 4 * x + z, 4 * lax.rem(x, 2) + z
    crossing = {}
    for k, device in xz_peers.items():
        theirs = 4 * lax.rem(x + k // 4, 2) + lax.rem(z + k, 4)
        slot = 4 * ((4 - k // 4) % 4) + (4 - k % 4) % 4
        crossing[k] = remote(
            own_half.at[:, eighth(theirs, y * 64)], by_xz.at[me], xz_send.at[k], xz_recv.at[slot], device
        )
    for copy in crossing.values():
        copy.start()
    by_xz[me] = own_half[:, eighth(group, y * 64)]

    for load in loads[2:]:
        load.wait()

    def update(step, carry):
        rows = pl.ds(pl.multiple_of(step * CHUNK, CHUNK), CHUNK)
        for c in range(2):
            for j in range(4):
                new_object[c, rows, part(j)] = old[c, rows, part(j)] + own[c, j, rows] * inverse[j, rows]
        return carry

    lax.fori_loop(0, 512 // CHUNK, update, 0)

    for copy in crossing.values():
        copy.wait_recv()
    total = by_xz[0]
    for k in range(1, 16):
        total += by_xz[k]
    illumination = total[4] + 1.0
    pixels = eighth(group, y * 64)
    lanes = pl.ds(pl.multiple_of(core * HALF, HALF), HALF)
    home = eighth(group, half_at + y * 64)
    for m in range(MODES):
        for c in range(2):
            turned[2 * m + c, home] = probe[m, c, pixels, lanes] + total[2 * m + c] / illumination

    back_xz = {
        k: remote(
            turned.at[:, home], turned.at[:, home],
            xz_back_send.at[k], xz_back_recv.at[4 * (k // 4) + (4 - k % 4) % 4], device,
        )
        for k, device in set_peers.items()
    }
    for copy in back_xz.values():
        copy.start()
    for copy in back_xz.values():
        copy.wait_recv()

    def quarter(d):
        return pl.ds(pl.multiple_of(half_at + lax.rem(y + d, 4) * 64, 64), 64)

    back_y = {
        d: remote(
            turned.at[:, quarter(0)], turned.at[:, quarter(0)], y_back_send.at[d - 1], y_back_recv.at[3 - d], y_peers[d]
        )
        for d in (1, 2, 3)
    }
    last = {
        d: remote(turned.at[:, quarter(d)], turned.at[:, quarter(d)], last_send.at[d], last_recv.at[d], sibling)
        for d in range(4)
    }
    for d in (1, 2, 3):
        back_y[d].start()
    last[0].start()
    for d in (1, 2, 3):
        back_y[4 - d].wait_recv()
        last[d].start()

    @pl.when(has_above)
    def _():
        lower.wait_recv()

        def add(step, carry):
            rows = pl.ds(pl.multiple_of(step * CHUNK, CHUNK), CHUNK)
            for c in range(2):
                for j in range(4):
                    new_object[c, rows, part(j)] += below_in[c, j, rows] * inverse[j, rows]
            return carry

        lax.fori_loop(0, SIDE // CHUNK, add, 0)

    @pl.when(has_left)
    def _():
        right_lower.wait_recv()
        right_upper.wait_recv()

        def add(step, carry):
            rows = pl.ds(pl.multiple_of(step * CHUNK, CHUNK), CHUNK)
            for c in range(2):
                for j in range(2):
                    new_object[c, rows, part(j)] += right_in[c, j, rows] * inverse[j, rows]
            return carry

        lax.fori_loop(0, 512 // CHUNK, add, 0)

    for d in range(4):
        last[d].wait_recv()
    pl.when(has_below)(corner.wait_send)
    pl.when(has_below)(lower.wait_send)
    pl.when(has_right)(right_lower.wait_send)
    pl.when(has_right)(right_upper.wait_send)
    for copies in (halves, outward, crossing, back_xz, back_y, last):
        for copy in copies.values():
            copy.wait_send()


def finish(grid, probe_sum, tile, inverse_light, probe):
    vmem, anywhere = [pl.BlockSpec(memory_space=space) for space in (pltpu.VMEM, pl.ANY)]
    f32 = functools.partial(pltpu.VMEM, dtype=jnp.float32)
    dma = pltpu.SemaphoreType.DMA
    return pl.pallas_call(
        finish_kernel,
        out_shape=(
            jax.ShapeDtypeStruct(tile.shape, jnp.float32),
            jax.ShapeDtypeStruct((4, 2 * SIDE, HALF), jnp.float32),
        ),
        in_specs=[anywhere] * 4 + [vmem],
        out_specs=(vmem, vmem),
        scratch_shapes=[
            f32((2, 4, 512, HALF)),
            f32((5, 256, HALF)),
            f32((4, 512, HALF)),
            f32((2, 512, 512)),
            f32((2, 2, 256, HALF)),
            f32((2, 4, 256, HALF)),
            f32((2, 2, 512, HALF)),
            f32((2, 2, 256, HALF)),
            f32((5, 256, HALF)),
            f32((3, 5, 64, HALF)),
            f32((16, 5, 8, HALF)),
            dma((5,)), dma((4,)), dma((4,)), dma((4,)), dma((4,)),
            dma((3,)), dma((3,)), dma((16,)), dma((16,)), dma((8,)), dma((8,)), dma((3,)), dma((3,)), dma((4,)), dma((4,)),
        ],
        compiler_params=pltpu.CompilerParams(
            collective_id=0, has_side_effects=True, vmem_limit_bytes=VMEM_LIMIT
        ),
        name="finish",
    )(grid, probe_sum, tile, inverse_light, probe)


def publish_kernel(object_in, probe_in, new_object, new_probe):
    new_object[...] = object_in[...]
    for k in range(2 * MODES):
        for j in range(2):
            new_probe[k // 2, k % 2, :, part(j)] = probe_in[k, pl.ds(j * SIDE, SIDE)]


def publish(object_in, probe_in):
    vmem = pl.BlockSpec(memory_space=pltpu.VMEM)
    return pl.pallas_call(
        publish_kernel,
        out_shape=(
            jax.ShapeDtypeStruct(object_in.shape, jnp.float32),
            jax.ShapeDtypeStruct((MODES, 2, SIDE, SIDE), jnp.float32),
        ),
        in_specs=[vmem] * 2,
        out_specs=(vmem,) * 2,
        name="publish",
    )(object_in, probe_in)


def body(object_field, probe, amplitudes, positions, counts):
    right_rim, lower_rim, inverse_light, by_parity = rims(positions, counts, object_field, probe, amplitudes)
    grid, probe_sum = patterns(positions, counts, object_field, right_rim, lower_rim, probe, by_parity)
    return publish(*finish(grid, probe_sum, object_field, inverse_light, probe))


def solution(mesh):
    in_specs = (
        P(None, "row", "col"),
        P(),
        P(("row", "col"), None, None),
        P(("row", "col"), None),
        P(("row", "col")),
    )
    out_specs = (P(None, "row", "col"), P())
    return jax.shard_map(body, mesh=mesh, in_specs=in_specs, out_specs=out_specs, check_vma=False)
```

time: 134 us -> 112 us (0.84)
  Pallas kernels: 86.5 us -> 110 us
  waiting for transfers between devices: 16.9 us -> 0 us
  starting transfers between devices: 16.4 us -> 0 us
  local copies, waits for them, and re-layouts: 10.7 us -> 1.35 us
  other arithmetic: 1.51 us -> 0 us
    pallas_call x1 -> x2, Pallas kernels: 5.4 us -> 34.3 us  [the longest x1 30.7 us: rims(): pl.pallas_call(rims_kernel, out_shape=(jax.ShapeDtypeStruct((2, 2, 768, H...]
    ppermute x6 -> x0, waiting for transfers between devices: 16.9 us -> none  [the longest x4 16.2 us: shift_up(): return lax.ppermute(array, axis, [(i, i - 1) for i in range(1, count)])]
    ppermute x6 -> x0, starting transfers between devices: 16.4 us -> none  [the longest x4 8.98 us: shift_up(): return lax.ppermute(array, axis, [(i, i - 1) for i in range(1, count)])]
    pallas_call x1, Pallas kernels: 66.8 us -> 58.1 us  [finish(): pl.pallas_call(finish_kernel, out_shape=(jax.ShapeDtypeStruct(tile.shape,...]
    unnamed x11 -> x1, local copies, waits for them, and re-layouts: 5.4 us -> 1.35 us
    slice x4 -> x0, local copies, waits for them, and re-layouts: 3.13 us -> none  [the longest x1 2.28 us: body(): right_lower = shift_up(object_field[:, SIDE:, :SIDE], 'col')]
    pallas_call x1, Pallas kernels: 14.3 us -> 17.1 us  [patterns(): pl.pallas_call(pattern_kernel, out_shape=(jax.ShapeDtypeStruct((2, 6, 768...]
  transfers between devices with their start and end apart: 6 -> 0, of which waited for: 3 -> 0; matrix products, arithmetic and copies ran while one was open for 4% -> 0% of each run, Pallas kernels for 4% -> 0%
where the time goes in v1:
time: 112 us
  Pallas kernels  110 us (98%)
  local copies, waits for them, and re-layouts  1.35 us (1%)
  between operations  1.3 us (1%)
    pallas_call x1, Pallas kernels, finish(): pl.pallas_call(finish_kernel, out_shape=(jax.ShapeDtypeStruct(tile.shape,...  58.1 us
    pallas_call x1, Pallas kernels, rims(): pl.pallas_call(rims_kernel, out_shape=(jax.ShapeDtypeStruct((2, 2, 768, H...  30.7 us
    pallas_call x1, Pallas kernels, patterns(): pl.pallas_call(pattern_kernel, out_shape=(jax.ShapeDtypeStruct((2, 6, 768...  17.1 us
    pallas_call x1, Pallas kernels, publish(): pl.pallas_call(publish_kernel, out_shape=(jax.ShapeDtypeStruct(object_in....  3.65 us

profile of v1, /device:TPU:1, one launch (start us, length us, event | category | flops | bytes accessed | tf_op | source)
XLA Modules:
  0.0 112.2 jit_solution(2274048600509793594)
XLA Ops:
  1.3 1.3 %copy.9.positions = s32[8,2]{1,0:T(8,128)} copy(s32[8,2]{0,1:T(2,128)} %param.9) | data formatting | bytes 128 | tf_op args[3]
  2.6 30.7 %rims.1 = (f32[2,2,768,128]{3,2,1,0:T(8,128)}, f32[2,4,256,128]{3,2,1,0:T(8,128)}, f32[4,512,128]{2,1,0:T(8,128)}, f32[8,256,256]{2,1,0:T(8,128)}) custom-call(s32[8,2]{1,0:T(8,128)} %copy.9.positions, s32[1]{0:T(128)S(6)} %copy.10.counts, f32[2,512,512]{2,1,0:T(8,128)} %tile.5, f32[2,2,256,256]{3,2,1,0:T(8,128)} %probe.3, f32[8,256,256]{2,1,0:T(8,128)} %amplitude.1), custom_call_target="tpu_custom_call" | custom-call | tf_op jit(solution)/shard_map/rims/pallas_call | solution.py:464
  33.3 17.1 %patterns.1 = (f32[2,6,768,128]{3,2,1,0:T(8,128)}, f32[5,512,128]{2,1,0:T(8,128)}) custom-call(s32[8,2]{1,0:T(8,128)} %copy.9.positions, s32[1]{0:T(128)S(6)} %copy.10.counts, f32[2,512,512]{2,1,0:T(8,128)} %tile.5, f32[2,2,768,128]{3,2,1,0:T(8,128)} %get-tuple-element.10.right_rim, f32[2,4,256,128]{3,2,1,0:T(8,128)} %get-tuple-element.11.lower_rim, ...), custom_call_target="tpu_custom_call" | custom-call | flops 5000000000 | bytes 20000000 | tf_op jit(solution)/shard_map/patterns/pallas_call | solution.py:234
  50.4 58.1 %finish.1 = (f32[2,512,512]{2,1,0:T(8,128)}, f32[4,512,128]{2,1,0:T(8,128)}) custom-call(f32[2,6,768,128]{3,2,1,0:T(8,128)} %get-tuple-element.13.grid, f32[5,512,128]{2,1,0:T(8,128)} %get-tuple-element.14.probe_sum, f32[2,512,512]{2,1,0:T(8,128)} %tile.5, f32[4,512,128]{2,1,0:T(8,128)} %get-tuple-element.15.inverse_light, f32[2,2,256,256]{3,2,1,0:T(8,128)} %probe.3), custom_call_target="tpu_custom_call" | custom-call | tf_op jit(solution)/shard_map/finish/pallas_call | solution.py:704
  108.5 3.7 %publish.1 = (f32[2,512,512]{2,1,0:T(8,128)}, f32[2,2,256,256]{3,2,1,0:T(8,128)}) custom-call(f32[2,512,512]{2,1,0:T(8,128)} %get-tuple-element.16.object_in, f32[4,512,128]{2,1,0:T(8,128)} %get-tuple-element.17.probe_in), custom_call_target="tpu_custom_call" | custom-call | tf_op jit(solution)/shard_map/publish/pallas_call | solution.py:743

commit v2 on v1

--- a/solution.py
+++ b/solution.py
@@ -69,8 +69,8 @@
     row_start, col_start = lax.axis_index("row") * 512, lax.axis_index("col") * 512
 
     def phases(slot, live, patch, rows_in, rows_out, columns_in, columns_out):
-        top = positions[slot, 0] - row_start
-        left = positions[slot, 1] - col_start
+        top = positions[0, slot] - row_start
+        left = positions[1, slot] - col_start
         first = left // HALF
         shift = lax.rem(left, HALF)
         back_shift = lax.rem(HALF - shift, HALF)
@@ -269,8 +269,8 @@
 
 
 def rims_kernel(
-    positions, counts, tile, probe, amplitude, right_rim, lower_rim, inverse_light, by_parity,
-    parity, canvas, light, measured, reordered, columns, scan_in, scan, local_sems,
+    positions, counts, tile, probe_in, amplitude, right_rim, lower_rim, inverse_light, by_parity,
+    probe, parity, canvas, light, measured, reordered, columns, scan_in, scan, local_sems,
     upper_send, upper_recv, under_send, under_recv, lower_send, lower_recv, corner_send, corner_recv,
     scan_send, scan_recv,
 ):
@@ -291,12 +291,14 @@
 
     load = pltpu.make_async_copy(amplitude, measured, local_sems.at[1])
     load.start()
+    probe_load = pltpu.make_async_copy(probe_in, probe, local_sems.at[0])
+    probe_load.start()
     slot_of = lax.broadcasted_iota(jnp.int32, (8, HALF), 0)
     field = lax.broadcasted_iota(jnp.int32, (8, HALF), 1)
     own_scan = jnp.where(slot_of < counts[0], 1, 0)
     for slot in range(8):
         for k in range(2):
-            own_scan = jnp.where((slot_of == slot) & (field == k), positions[slot, k], own_scan)
+            own_scan = jnp.where((slot_of == slot) & (field == k), positions[k, slot], own_scan)
     scan_in[0] = own_scan
     pl.semaphore_wait(barrier, sum(there.astype(jnp.int32) for there, _ in partners))
 
@@ -376,6 +378,7 @@
     stores[0].start()
 
     canvas[...] = jnp.zeros_like(canvas)
+    probe_load.wait()
     for j in range(2):
         canvas[4 + j, pl.ds(512, SIDE), :] = sum(probe[m, c, :, part(j)] * probe[m, c, :, part(j)] for m in range(MODES) for c in range(2))
     light[...] = jnp.zeros_like(light)
@@ -458,7 +461,7 @@
 
 
 def rims(positions, counts, tile, probe, amplitude):
-    smem, vmem, anywhere = [pl.BlockSpec(memory_space=space) for space in (pltpu.SMEM, pltpu.VMEM, pl.ANY)]
+    smem, anywhere = [pl.BlockSpec(memory_space=space) for space in (pltpu.SMEM, pl.ANY)]
     f32 = functools.partial(pltpu.VMEM, dtype=jnp.float32)
     dma = pltpu.SemaphoreType.DMA
     return pl.pallas_call(
@@ -469,9 +472,10 @@
             jax.ShapeDtypeStruct((4, 512, HALF), jnp.float32),
             jax.ShapeDtypeStruct(amplitude.shape, jnp.float32),
         ),
-        in_specs=[smem, smem, anywhere, vmem, anywhere],
+        in_specs=[smem, smem, anywhere, anywhere, anywhere],
         out_specs=(anywhere,) * 4,
         scratch_shapes=[
+            f32(probe.shape),
             pltpu.VMEM((3 * SIDE, SIDE), jnp.bfloat16),
             f32((13, 1536, HALF)),
             f32((4, 512, HALF)),
@@ -491,22 +495,25 @@
 
 
 def finish_kernel(
-    grid, probe_sum, tile, inverse_light, probe, new_object, turned,
-    own, own_half, inverse, old, corner_in, below_in, right_in, right_out, half_in, by_y, by_xz,
-    local_sems, spill_send, spill_recv, half_send, half_recv, y_send, y_recv, xz_send, xz_recv,
-    xz_back_send, xz_back_recv, y_back_send, y_back_recv, last_send, last_recv,
+    grid, probe_sum, tile, inverse_light, probe_in, new_object, turned,
+    probe, own, own_half, inverse, old, corner_in, below_in, right_in, right_out, half_in, by_big, by_cross,
+    local_sems, corner_send, corner_recv, right_send, right_recv, below_send, below_recv, half_send, half_recv, big_send, big_recv, cross_send, cross_recv,
+    cross_back_send, cross_back_recv, big_back_send, big_back_recv, last_send, last_recv,
 ):
     row, col = lax.axis_index("row"), lax.axis_index("col")
     x, core = row // 2, lax.rem(row, 2)
     y, z = col // 4, lax.rem(col, 4)
     sibling = (row + 1 - 2 * core, col)
-    y_peers = {d: (row, lax.rem(y + d, 4) * 4 + z) for d in (1, 2, 3)}
-    xz_peers = {4 * dx + dz: (lax.rem(x + dx, 4) * 2 + core, y * 4 + lax.rem(z + dz, 4)) for dx in range(4) for dz in range(4)}
-    del xz_peers[0]
-    twin = x + 1 - 2 * lax.rem(x, 2)
-    set_peers = {
-        4 * flip + dz: ((twin if flip else x) * 2 + core, y * 4 + lax.rem(z + dz, 4)) for flip in range(2) for dz in range(4)
-    }
+    big, other = x, y
+
+    def at(b, o, c):
+        return (b * 2 + core, o * 4 + c)
+
+    big_peers = {d: at(lax.rem(big + d, 4), other, z) for d in (1, 2, 3)}
+    cross_peers = {4 * d + dz: at(big, lax.rem(other + d, 4), lax.rem(z + dz, 4)) for d in range(4) for dz in range(4)}
+    del cross_peers[0]
+    twin = other + 1 - 2 * lax.rem(other, 2)
+    set_peers = {4 * flip + dz: at(big, twin if flip else other, lax.rem(z + dz, 4)) for flip in range(2) for dz in range(4)}
     del set_peers[0]
     has_above, has_below = row > 0, row < 7
     has_left, has_right = col > 0, col < 15
@@ -521,12 +528,13 @@
         pltpu.make_async_copy(grid.at[:, pl.ds(0, 4), pl.ds(0, 512)], own, local_sems.at[2]),
         pltpu.make_async_copy(inverse_light, inverse, local_sems.at[3]),
         pltpu.make_async_copy(tile, old, local_sems.at[4]),
+        pltpu.make_async_copy(probe_in, probe, local_sems.at[5]),
     ]
     for load in loads:
         load.start()
 
     barrier = pltpu.get_barrier_semaphore()
-    for device in [sibling, *y_peers.values(), *xz_peers.values()]:
+    for device in [sibling, *big_peers.values(), *cross_peers.values()]:
         signal(device)
     steps = ((has_above, (row - 1, col)), (has_below, (row + 1, col)), (has_left, (row, col - 1)), (has_right, (row, col + 1)))
     for there, device in steps:
@@ -535,42 +543,50 @@
 
     below, right = (row + 1, col), (row, col + 1)
     corner = remote(
-        grid.at[:, pl.ds(4, 2), pl.ds(512, 256)], corner_in, spill_send.at[0], spill_recv.at[0], below
+        grid.at[:, pl.ds(4, 2), pl.ds(512, 256)], corner_in, corner_send.at[0], corner_recv.at[0], below
     )
-    right_lower = remote(
-        grid.at[:, pl.ds(4, 2), pl.ds(256, 256)], right_in.at[:, :, pl.ds(256, 256)],
-        spill_send.at[1], spill_recv.at[1], right,
-    )
-    lower = remote(grid.at[:, pl.ds(0, 4), pl.ds(512, 256)], below_in, spill_send.at[2], spill_recv.at[2], below)
-    right_upper = remote(
-        right_out, right_in.at[:, :, pl.ds(0, 256)], spill_send.at[3], spill_recv.at[3], right
-    )
-
-    def y_rows(d):
-        return pl.ds(pl.multiple_of(lax.rem(y + d, 4) * 64, 64), 64)
+    to_right = []
+    for k in range(4):
+        rows = pl.ds(128 * k, 128)
+        source = right_out.at[:, :, rows] if k < 2 else grid.at[:, pl.ds(4, 2), rows]
+        to_right.append(remote(source, right_in.at[:, :, rows], right_send.at[k], right_recv.at[k], right))
+    to_below = []
+    for k in range(2):
+        to_below.append(
+            remote(
+                grid.at[:, pl.ds(0, 4), pl.ds(512 + 128 * k, 128)], below_in.at[:, :, pl.ds(128 * k, 128)],
+                below_send.at[k], below_recv.at[k], below,
+            )
+        )
+
+    def big_rows(d):
+        return pl.ds(pl.multiple_of(lax.rem(big + d, 4) * 64, 64), 64)
 
     halves = {
         d: remote(
-            probe_sum.at[:, pl.ds(pl.multiple_of((1 - core) * 256 + lax.rem(y + d, 4) * 64, 64), 64)],
-            half_in.at[:, y_rows(d)], half_send.at[d], half_recv.at[d], sibling,
+            probe_sum.at[:, pl.ds(pl.multiple_of((1 - core) * 256 + lax.rem(big + d, 4) * 64, 64), 64)],
+            half_in.at[:, big_rows(d)], half_send.at[d], half_recv.at[d], sibling,
         )
         for d in range(4)
     }
     pl.when(has_below)(corner.start)
     for d in (2, 1, 3, 0):
         halves[d].start()
-    pl.when(has_right)(right_lower.start)
+    pl.when(has_right)(to_right[2].start)
+    pl.when(has_right)(to_right[3].start)
 
     loads[0].wait()
     outward = {
-        d: remote(own_half.at[:, y_rows(d)], by_y.at[3 - d], y_send.at[d - 1], y_recv.at[3 - d], y_peers[d])
+        d: remote(own_half.at[:, big_rows(d)], by_big.at[3 - d], big_send.at[d - 1], big_recv.at[3 - d], big_peers[d])
         for d in (1, 2, 3)
     }
     for d in (2, 1, 3, 0):
         halves[d].wait_recv()
-        own_half[:, y_rows(d)] = own_half[:, y_rows(d)] + half_in[:, y_rows(d)]
+        own_half[:, big_rows(d)] = own_half[:, big_rows(d)] + half_in[:, big_rows(d)]
         if d:
             outward[d].start()
+    pl.when(has_below)(to_below[0].start)
+    pl.when(has_below)(to_below[1].start)
 
     loads[1].wait()
 
@@ -579,28 +595,27 @@
         corner.wait_recv()
         right_out[...] = right_out[...] + corner_in[...]
 
-    pl.when(has_right)(right_upper.start)
-    pl.when(has_below)(lower.start)
 
     for d in (1, 2, 3):
         outward[d].wait_recv()
-    mine = y_rows(0)
-    own_half[:, mine] = own_half[:, mine] + (by_y[0] + by_y[1] + by_y[2])
+    mine = big_rows(0)
+    own_half[:, mine] = own_half[:, mine] + (by_big[0] + by_big[1] + by_big[2])
 
     def eighth(index, base):
         return pl.ds(pl.multiple_of(base + index * 8, 8), 8)
 
-    me, group = 4 * x + z, 4 * lax.rem(x, 2) + z
+    me, group = 4 * other + z, 4 * lax.rem(other, 2) + z
     crossing = {}
-    for k, device in xz_peers.items():
-        theirs = 4 * lax.rem(x + k // 4, 2) + lax.rem(z + k, 4)
+    for k, device in cross_peers.items():
+        theirs = 4 * lax.rem(other + k // 4, 2) + lax.rem(z + k, 4)
         slot = 4 * ((4 - k // 4) % 4) + (4 - k % 4) % 4
         crossing[k] = remote(
-            own_half.at[:, eighth(theirs, y * 64)], by_xz.at[me], xz_send.at[k], xz_recv.at[slot], device
+            own_half.at[:, eighth(theirs, big * 64)], by_cross.at[me], cross_send.at[k], cross_recv.at[slot], device
         )
     for copy in crossing.values():
         copy.start()
-    by_xz[me] = own_half[:, eighth(group, y * 64)]
+    pl.when(has_right)(to_right[0].start)
+    by_cross[me] = own_half[:, eighth(group, big * 64)]
 
     for load in loads[2:]:
         load.wait()
@@ -616,35 +631,36 @@
 
     for copy in crossing.values():
         copy.wait_recv()
-    total = by_xz[0]
+    total = by_cross[0]
     for k in range(1, 16):
-        total += by_xz[k]
+        total += by_cross[k]
     illumination = total[4] + 1.0
-    pixels = eighth(group, y * 64)
+    pixels = eighth(group, big * 64)
     lanes = pl.ds(pl.multiple_of(core * HALF, HALF), HALF)
-    home = eighth(group, half_at + y * 64)
+    home = eighth(group, half_at + big * 64)
     for m in range(MODES):
         for c in range(2):
             turned[2 * m + c, home] = probe[m, c, pixels, lanes] + total[2 * m + c] / illumination
 
-    back_xz = {
+    back_cross = {
         k: remote(
             turned.at[:, home], turned.at[:, home],
-            xz_back_send.at[k], xz_back_recv.at[4 * (k // 4) + (4 - k % 4) % 4], device,
+            cross_back_send.at[k], cross_back_recv.at[4 * (k // 4) + (4 - k % 4) % 4], device,
         )
         for k, device in set_peers.items()
     }
-    for copy in back_xz.values():
+    for copy in back_cross.values():
         copy.start()
-    for copy in back_xz.values():
+    pl.when(has_right)(to_right[1].start)
+    for copy in back_cross.values():
         copy.wait_recv()
 
     def quarter(d):
-        return pl.ds(pl.multiple_of(half_at + lax.rem(y + d, 4) * 64, 64), 64)
-
-    back_y = {
+        return pl.ds(pl.multiple_of(half_at + lax.rem(big + d, 4) * 64, 64), 64)
+
+    back_big = {
         d: remote(
-            turned.at[:, quarter(0)], turned.at[:, quarter(0)], y_back_send.at[d - 1], y_back_recv.at[3 - d], y_peers[d]
+            turned.at[:, quarter(0)], turned.at[:, quarter(0)], big_back_send.at[d - 1], big_back_recv.at[3 - d], big_peers[d]
         )
         for d in (1, 2, 3)
     }
@@ -653,15 +669,16 @@
         for d in range(4)
     }
     for d in (1, 2, 3):
-        back_y[d].start()
+        back_big[d].start()
     last[0].start()
     for d in (1, 2, 3):
-        back_y[4 - d].wait_recv()
+        back_big[4 - d].wait_recv()
         last[d].start()
 
     @pl.when(has_above)
     def _():
-        lower.wait_recv()
+        for copy in to_below:
+            copy.wait_recv()
 
         def add(step, carry):
             rows = pl.ds(pl.multiple_of(step * CHUNK, CHUNK), CHUNK)
@@ -674,8 +691,8 @@
 
     @pl.when(has_left)
     def _():
-        right_lower.wait_recv()
-        right_upper.wait_recv()
+        for copy in to_right:
+            copy.wait_recv()
 
         def add(step, carry):
             rows = pl.ds(pl.multiple_of(step * CHUNK, CHUNK), CHUNK)
@@ -689,10 +706,11 @@
     for d in range(4):
         last[d].wait_recv()
     pl.when(has_below)(corner.wait_send)
-    pl.when(has_below)(lower.wait_send)
-    pl.when(has_right)(right_lower.wait_send)
-    pl.when(has_right)(right_upper.wait_send)
-    for copies in (halves, outward, crossing, back_xz, back_y, last):
+    for copy in to_below:
+        pl.when(has_below)(copy.wait_send)
+    for copy in to_right:
+        pl.when(has_right)(copy.wait_send)
+    for copies in (halves, outward, crossing, back_cross, back_big, last):
         for copy in copies.values():
             copy.wait_send()
 
@@ -707,9 +725,10 @@
             jax.ShapeDtypeStruct(tile.shape, jnp.float32),
             jax.ShapeDtypeStruct((4, 2 * SIDE, HALF), jnp.float32),
         ),
-        in_specs=[anywhere] * 4 + [vmem],
+        in_specs=[anywhere] * 5,
         out_specs=(vmem, vmem),
         scratch_shapes=[
+            f32(probe.shape),
             f32((2, 4, 512, HALF)),
             f32((5, 256, HALF)),
             f32((4, 512, HALF)),
@@ -721,7 +740,7 @@
             f32((5, 256, HALF)),
             f32((3, 5, 64, HALF)),
             f32((16, 5, 8, HALF)),
-            dma((5,)), dma((4,)), dma((4,)), dma((4,)), dma((4,)),
+            dma((6,)), dma((1,)), dma((1,)), dma((4,)), dma((4,)), dma((2,)), dma((2,)), dma((4,)), dma((4,)),
             dma((3,)), dma((3,)), dma((16,)), dma((16,)), dma((8,)), dma((8,)), dma((3,)), dma((3,)), dma((4,)), dma((4,)),
         ],
         compiler_params=pltpu.CompilerParams(
@@ -753,6 +772,7 @@
 
 
 def body(object_field, probe, amplitudes, positions, counts):
+    positions = positions.T
     right_rim, lower_rim, inverse_light, by_parity = rims(positions, counts, object_field, probe, amplitudes)
     grid, probe_sum = patterns(positions, counts, object_field, right_rim, lower_rim, probe, by_parity)
     return publish(*finish(grid, probe_sum, object_field, inverse_light, probe))

time: 112 us -> 106 us (0.946)
  the two profiles are of different devices: /device:TPU:1 before, /device:TPU:17 now
where the time goes in v2:
time: 106 us
  Pallas kernels  105 us (99%)
  between operations  1.3 us (1%)
    pallas_call x1, Pallas kernels, finish(): pl.pallas_call(finish_kernel, out_shape=(jax.ShapeDtypeStruct(tile.shape,...  59.9 us
    pallas_call x1, Pallas kernels, rims(): pl.pallas_call(rims_kernel, out_shape=(jax.ShapeDtypeStruct((2, 2, 768, H...  29.4 us
    pallas_call x1, Pallas kernels, patterns(): pl.pallas_call(pattern_kernel, out_shape=(jax.ShapeDtypeStruct((2, 6, 768...  12 us
    pallas_call x1, Pallas kernels, publish(): pl.pallas_call(publish_kernel, out_shape=(jax.ShapeDtypeStruct(object_in....  3.65 us

profile of v2, /device:TPU:17, one launch (start us, length us, event | category | flops | bytes accessed | tf_op | source)
XLA Modules:
  0.0 106.2 jit_solution(7291676205025120787)
XLA Ops:
  1.3 29.4 %rims.1 = (f32[2,2,768,128]{3,2,1,0:T(8,128)}, f32[2,4,256,128]{3,2,1,0:T(8,128)}, f32[4,512,128]{2,1,0:T(8,128)}, f32[8,256,256]{2,1,0:T(8,128)}) custom-call(s32[2,8]{1,0:T(2,128)} %bitcast.1, s32[1]{0:T(128)S(6)} %copy.8.counts, f32[2,512,512]{2,1,0:T(8,128)} %tile.5, f32[2,2,256,256]{3,2,1,0:T(8,128)} %probe_in.5, f32[8,256,256]{2,1,0:T(8,128)} %amplitude.1), custom_call_target="tpu_custom_call" | custom-call | tf_op jit(solution)/shard_map/rims/pallas_call | solution.py:467
  30.7 12.0 %patterns.1 = (f32[2,6,768,128]{3,2,1,0:T(8,128)}, f32[5,512,128]{2,1,0:T(8,128)}) custom-call(s32[2,8]{1,0:T(2,128)} %bitcast.2, s32[1]{0:T(128)S(6)} %copy.8.counts, f32[2,512,512]{2,1,0:T(8,128)} %tile.5, f32[2,2,768,128]{3,2,1,0:T(8,128)} %get-tuple-element.10.right_rim, f32[2,4,256,128]{3,2,1,0:T(8,128)} %get-tuple-element.11.lower_rim, ...), custom_call_target="tpu_custom_call" | custom-call | flops 5000000000 | bytes 20000000 | tf_op jit(solution)/shard_map/patterns/pallas_call | solution.py:234
  42.7 59.9 %finish.1 = (f32[2,512,512]{2,1,0:T(8,128)}, f32[4,512,128]{2,1,0:T(8,128)}) custom-call(f32[2,6,768,128]{3,2,1,0:T(8,128)} %get-tuple-element.13.grid, f32[5,512,128]{2,1,0:T(8,128)} %get-tuple-element.14.probe_sum, f32[2,512,512]{2,1,0:T(8,128)} %tile.5, f32[4,512,128]{2,1,0:T(8,128)} %get-tuple-element.15.inverse_light, f32[2,2,256,256]{3,2,1,0:T(8,128)} %probe_in.5), custom_call_target="tpu_custom_call" | custom-call | tf_op jit(solution)/shard_map/finish/pallas_call | solution.py:722
  102.6 3.7 %publish.1 = (f32[2,512,512]{2,1,0:T(8,128)}, f32[2,2,256,256]{3,2,1,0:T(8,128)}) custom-call(f32[2,512,512]{2,1,0:T(8,128)} %get-tuple-element.16.object_in, f32[4,512,128]{2,1,0:T(8,128)} %get-tuple-element.17.probe_in), custom_call_target="tpu_custom_call" | custom-call | tf_op jit(solution)/shard_map/publish/pallas_call | solution.py:762

commit v3 on v2

--- a/solution.py
+++ b/solution.py
@@ -585,8 +585,6 @@
         own_half[:, big_rows(d)] = own_half[:, big_rows(d)] + half_in[:, big_rows(d)]
         if d:
             outward[d].start()
-    pl.when(has_below)(to_below[0].start)
-    pl.when(has_below)(to_below[1].start)
 
     loads[1].wait()
 
@@ -615,6 +613,8 @@
     for copy in crossing.values():
         copy.start()
     pl.when(has_right)(to_right[0].start)
+    pl.when(has_below)(to_below[0].start)
+    pl.when(has_below)(to_below[1].start)
     by_cross[me] = own_half[:, eighth(group, big * 64)]
 
     for load in loads[2:]:

time: 106 us -> 103 us (0.972)
  Pallas kernels: 105 us -> 102 us
    pallas_call x1, Pallas kernels: 59.9 us -> 51.7 us  [finish(): pl.pallas_call(finish_kernel, out_shape=(jax.ShapeDtypeStruct(tile.shape,...]
    pallas_call x1, Pallas kernels: 12 us -> 17 us  [patterns(): pl.pallas_call(pattern_kernel, out_shape=(jax.ShapeDtypeStruct((2, 6, 768...]
where the time goes in v3:
time: 103 us
  Pallas kernels  102 us (99%)
  between operations  1.3 us (1%)
    pallas_call x1, Pallas kernels, finish(): pl.pallas_call(finish_kernel, out_shape=(jax.ShapeDtypeStruct(tile.shape,...  51.7 us
    pallas_call x1, Pallas kernels, rims(): pl.pallas_call(rims_kernel, out_shape=(jax.ShapeDtypeStruct((2, 2, 768, H...  29.4 us
    pallas_call x1, Pallas kernels, patterns(): pl.pallas_call(pattern_kernel, out_shape=(jax.ShapeDtypeStruct((2, 6, 768...  17 us
    pallas_call x1, Pallas kernels, publish(): pl.pallas_call(publish_kernel, out_shape=(jax.ShapeDtypeStruct(object_in....  3.65 us

profile of v3, /device:TPU:17, one launch (start us, length us, event | category | flops | bytes accessed | tf_op | source)
XLA Modules:
  0.0 103.1 jit_solution(15865693797242168248)
XLA Ops:
  1.3 29.4 %rims.1 = (f32[2,2,768,128]{3,2,1,0:T(8,128)}, f32[2,4,256,128]{3,2,1,0:T(8,128)}, f32[4,512,128]{2,1,0:T(8,128)}, f32[8,256,256]{2,1,0:T(8,128)}) custom-call(s32[2,8]{1,0:T(2,128)} %bitcast.1, s32[1]{0:T(128)S(6)} %copy.8.counts, f32[2,512,512]{2,1,0:T(8,128)} %tile.5, f32[2,2,256,256]{3,2,1,0:T(8,128)} %probe_in.5, f32[8,256,256]{2,1,0:T(8,128)} %amplitude.1), custom_call_target="tpu_custom_call" | custom-call | tf_op jit(solution)/shard_map/rims/pallas_call | solution.py:467
  30.7 17.0 %patterns.1 = (f32[2,6,768,128]{3,2,1,0:T(8,128)}, f32[5,512,128]{2,1,0:T(8,128)}) custom-call(s32[2,8]{1,0:T(2,128)} %bitcast.2, s32[1]{0:T(128)S(6)} %copy.8.counts, f32[2,512,512]{2,1,0:T(8,128)} %tile.5, f32[2,2,768,128]{3,2,1,0:T(8,128)} %get-tuple-element.10.right_rim, f32[2,4,256,128]{3,2,1,0:T(8,128)} %get-tuple-element.11.lower_rim, ...), custom_call_target="tpu_custom_call" | custom-call | flops 5000000000 | bytes 20000000 | tf_op jit(solution)/shard_map/patterns/pallas_call | solution.py:234
  47.7 51.7 %finish.1 = (f32[2,512,512]{2,1,0:T(8,128)}, f32[4,512,128]{2,1,0:T(8,128)}) custom-call(f32[2,6,768,128]{3,2,1,0:T(8,128)} %get-tuple-element.13.grid, f32[5,512,128]{2,1,0:T(8,128)} %get-tuple-element.14.probe_sum, f32[2,512,512]{2,1,0:T(8,128)} %tile.5, f32[4,512,128]{2,1,0:T(8,128)} %get-tuple-element.15.inverse_light, f32[2,2,256,256]{3,2,1,0:T(8,128)} %probe_in.5), custom_call_target="tpu_custom_call" | custom-call | tf_op jit(solution)/shard_map/finish/pallas_call | solution.py:722
  99.4 3.7 %publish.1 = (f32[2,512,512]{2,1,0:T(8,128)}, f32[2,2,256,256]{3,2,1,0:T(8,128)}) custom-call(f32[2,512,512]{2,1,0:T(8,128)} %get-tuple-element.16.object_in, f32[4,512,128]{2,1,0:T(8,128)} %get-tuple-element.17.probe_in), custom_call_target="tpu_custom_call" | custom-call | tf_op jit(solution)/shard_map/publish/pallas_call | solution.py:762
